TPU v7x, 128 devices: a whole 4x4x4 slice. The times are simulated.
128 devices in a mesh: gx: 16 (over y_hi, x, core), gy: 8 (over z, y_lo).
Axes of the slice: x: 4, y: 4 (y_hi: 2, y_lo: 2; y = y_hi * 2 + y_lo), z: 4, core: 2. Of those that a mesh axis runs over, the one named last changes fastest.
Arguments:
- control: float32 [16, 1024, 2048], P(None, 'gx', 'gy'), may hold values from -6 to 6
- sigma: float32 [16, 1024, 2048], P(None, 'gx', 'gy'), may hold values from 0.5 to 4
- vert_diff: float32 [15, 1024, 2048], P(None, 'gx', 'gy'), may hold values from 0.1 to 10
- zonal_diff: float32 [1024, 2048], P('gx', 'gy'), may hold values from 0.1 to 0.24
- merid_diff: float32 [1024, 2048], P('gx', 'gy'), may hold values from 0.1 to 0.24
- ocean_mask: int32 [1024, 2048], P('gx', 'gy'), may hold values from 0 to 1
- owner: int32 [262144, 1], P(('gx', 'gy')), may hold values from 0 to 127; in each aligned block of 2048 rows (0 to 2047, 2048 to 4095, ...) at most 64 rows name the same one
- cell: int32 [262144], P(('gx', 'gy')), may hold values from 0 to 16126, as said below
- interp_weights: float32 [4, 262144], P(None, ('gx', 'gy')), may hold values from 0 to 1, as said below
- innovation: float32 [16, 262144], P(None, ('gx', 'gy')), may hold values from -6 to 6
- obs_weight: float32 [16, 262144], P(None, ('gx', 'gy')), may hold values from 0.25 to 4
Outputs:
- increment: float32 [16, 1024, 2048], P(None, 'gx', 'gy')
- departures: float32 [16, 262144], P(None, ('gx', 'gy'))
- gradient: float32 [16, 1024, 2048], P(None, 'gx', 'gy')
Inputs may be any that keep to these rules, and one draw needn't show every extreme that they name: Among the profiles stored on one device, at most 64 name any one owner; every device is named by some profile. c = a * 256 + b names cell (a, b) of the owner's block of 64 x 256 cells with a <= 62 and b <= 254, so all four corners lie in that block. `interp_weights`: the four weights of a profile are the products of (1 - s, s) and (1 - t, t) for offsets s, t in [0, 1], corner order (a, b), (a + 1, b), (a, b + 1), (a + 1, b + 1).
All inputs are finite; a program needn't handle non-finite values.
Results may differ from a plain program's by a relative error of at most 0.00013.
Values sent between devices are 32-bit elements; how exact they have to be, the bound alone decides.
A program may use at most 128 MiB of HBM per device.

v0:
```python
import jax
import jax.numpy as jnp
from jax import lax
from jax.sharding import PartitionSpec as P

STEPS = 10


def extended_2(x, sides, width):
    for axis, dim in sides:
        size, length = (lax.axis_size(axis), x.shape[dim])
        up = [(i, (i + 1) % size) for i in range(size)]
        down = [(j, i) for i, j in up]
        last = lax.slice_in_dim(x, length - width, length, axis=dim)
        initial = lax.slice_in_dim(x, 0, width, axis=dim)
        before = lax.ppermute(last, axis, up)
        after = lax.ppermute(initial, axis, down)
        x = jnp.concatenate([before, x, after], axis=dim)
    return x


def thomas_factors(vert_diff):
    count = vert_diff.shape[0] + 1
    zero_plane = jnp.zeros_like(vert_diff[0])
    lower_diff = [zero_plane] + [vert_diff[level] for level in range(count - 1)]
    upper_diff = [vert_diff[level] for level in range(count - 1)] + [zero_plane]
    upper_factor = []
    inverse = []
    for level in range(count):
        diagonal = 1.0 + lower_diff[level] + upper_diff[level]
        if level > 0:
            diagonal = diagonal + lower_diff[level] * upper_factor[level - 1]
        pivot_inv = 1.0 / diagonal
        inverse.append(pivot_inv)
        upper_factor.append(-upper_diff[level] * pivot_inv)
    return (lower_diff, upper_factor, inverse)


def vertical_solve(rhs, lower_diff, upper_factor, inverse):
    count = rhs.shape[0]
    reduced = []
    for level in range(count):
        term = rhs[level]
        if level > 0:
            term = term + lower_diff[level] * reduced[level - 1]
        reduced.append(term * inverse[level])
    solution = [reduced[count - 1]]
    for level in range(count - 2, -1, -1):
        solution.insert(0, reduced[level] - upper_factor[level] * solution[0])
    return jnp.stack(solution)


def stencil(extended, face_x, face_y):
    centre = extended[:, 1:-1, 1:-1]
    east_flux = face_x[None, 1:-1, 1:-1] * (extended[:, 2:, 1:-1] - centre)
    west_flux = face_x[None, :-2, 1:-1] * (centre - extended[:, :-2, 1:-1])
    north_flux = face_y[None, 1:-1, 1:-1] * (extended[:, 1:-1, 2:] - centre)
    south_flux = face_y[None, 1:-1, :-2] * (centre - extended[:, 1:-1, :-2])
    return centre + east_flux - west_flux + north_flux - south_flux


def diffuse_all(field_start, face_x, face_y):

    def one_step(step_index, field_now):
        extended = extended_2(field_now, (("gx", 1), ("gy", 2)), 1)
        return stencil(extended, face_x, face_y)

    return lax.fori_loop(0, STEPS, one_step, field_start)


def interpolate(field_flat, corner_base, weights_flat, row_len):
    offsets = (0, row_len, 1, row_len + 1)
    model_vals = jnp.zeros((field_flat.shape[0], corner_base.shape[0]), jnp.float32)
    for corner in range(4):
        model_vals = (
            model_vals
            + weights_flat[corner][None, :] * field_flat[:, corner_base + offsets[corner]]
        )
    return model_vals


def slot_ranks(onehot):
    prof_count, devices = onehot.shape
    block = min(prof_count, 512)
    lower_tri = (jnp.arange(block)[:, None] >= jnp.arange(block)[None, :]).astype(jnp.float32)

    def count_block(carry, piece):
        inclusive = carry[None, :] + jnp.dot(
            lower_tri, piece, precision=lax.Precision.HIGHEST, preferred_element_type=jnp.float32
        )
        return (inclusive[-1], jnp.sum(inclusive * piece, axis=1))

    start_counts = jnp.zeros((devices,), jnp.float32)
    unused, ranks = lax.scan(
        count_block, start_counts, onehot.reshape(prof_count // block, block, devices)
    )
    return ranks.reshape(prof_count).astype(jnp.int32) - 1


def pack_slots(records, slot_index, buffer_len):
    width = min(buffer_len, 1024)
    starts = jnp.arange(buffer_len // width, dtype=jnp.int32) * width

    def place(start):
        placing = (
            slot_index[:, None] == start + jnp.arange(width, dtype=jnp.int32)[None, :]
        ).astype(jnp.float32)
        return jnp.dot(
            records, placing, precision=lax.Precision.HIGHEST, preferred_element_type=jnp.float32
        )

    blocks = lax.map(place, starts)
    return jnp.transpose(blocks, (1, 0, 2)).reshape(records.shape[0], buffer_len)


def unpack_slots(buffer, slot_index):
    rows, buffer_len = buffer.shape
    width = min(buffer_len, 1024)
    count = buffer_len // width
    pieces = jnp.transpose(buffer.reshape(rows, count, width), (1, 0, 2))

    def take(total, item):
        start, piece = item
        placing = (
            slot_index[:, None] == start + jnp.arange(width, dtype=jnp.int32)[None, :]
        ).astype(jnp.float32)
        term = lax.dot_general(
            piece,
            placing,
            (((1,), (1,)), ((), ())),
            precision=lax.Precision.HIGHEST,
            preferred_element_type=jnp.float32,
        )
        return (total + term, None)

    starts = jnp.arange(count, dtype=jnp.int32) * width
    total, unused = lax.scan(
        take, jnp.zeros((rows, slot_index.shape[0]), jnp.float32), (starts, pieces)
    )
    return total


def shards(
    control,
    sigma,
    vert_diff,
    zonal_diff,
    merid_diff,
    ocean_mask,
    owner,
    cell,
    interp_weights,
    innovation,
    obs_weight,
):
    levels, rows_x, rows_y = control.shape
    halo_width = 1
    wet_cells = ocean_mask.astype(jnp.float32)
    padded = extended_2(
        jnp.stack([zonal_diff, merid_diff, wet_cells]), (("gx", 1), ("gy", 2)), halo_width
    )
    total_y = lax.axis_size("gy") * rows_y
    merid_index = (
        lax.axis_index("gy") * rows_y
        - halo_width
        + jnp.arange(rows_y + 2 * halo_width, dtype=jnp.int32)
    )
    inside = ((merid_index >= 0) & (merid_index < total_y)).astype(jnp.float32)
    wet_wide = padded[2] * inside[None, :]
    east_wet = jnp.concatenate([wet_wide[1:], jnp.zeros_like(wet_wide[:1])], axis=0)
    north_wet = jnp.concatenate([wet_wide[:, 1:], jnp.zeros_like(wet_wide[:, :1])], axis=1)
    face_x = padded[0] * wet_wide * east_wet
    face_y = padded[1] * wet_wide * north_wet
    lower_diff, upper_factor, inverse = thomas_factors(vert_diff)
    masked_start = vertical_solve(wet_cells[None] * control, lower_diff, upper_factor, inverse)
    increment = sigma * diffuse_all(masked_start, face_x, face_y)
    devices = lax.axis_size("gx") * lax.axis_size("gy")
    prof_count = cell.shape[0]
    capacity = 4 * prof_count // devices
    buffer_len = devices * capacity
    target = owner[:, 0]
    onehot = (target[:, None] == jnp.arange(devices, dtype=jnp.int32)[None, :]).astype(jnp.float32)
    slot_index = target * capacity + slot_ranks(onehot)
    cell_float = cell.astype(jnp.float32)[None, :]
    field_flat = increment.reshape(levels, rows_x * rows_y)
    packed = pack_slots(
        jnp.concatenate([cell_float, interp_weights], axis=0), slot_index, buffer_len
    )
    cells_out = packed[0].astype(jnp.int32).reshape(1, devices, capacity)
    floats_out = packed[1:].reshape(4, devices, capacity)
    cells_in, weights_in = (
        lax.all_to_all(cells_out, ("gx", "gy"), split_axis=1, concat_axis=1, tiled=True),
        lax.all_to_all(floats_out, ("gx", "gy"), split_axis=1, concat_axis=1, tiled=True),
    )
    corner_base = jnp.maximum(cells_in.reshape(buffer_len), 0)
    weights_flat = weights_in.reshape(4, buffer_len)
    model_vals = interpolate(field_flat, corner_base, weights_flat, rows_y)
    returned = lax.all_to_all(
        model_vals.reshape(levels, devices, capacity),
        ("gx", "gy"),
        split_axis=1,
        concat_axis=1,
        tiled=True,
    )
    departures = unpack_slots(returned.reshape(levels, buffer_len), slot_index) - innovation
    weighted = obs_weight * departures
    weighted_out = pack_slots(weighted, slot_index, buffer_len).reshape(levels, devices, capacity)
    forcing = lax.all_to_all(
        weighted_out, ("gx", "gy"), split_axis=1, concat_axis=1, tiled=True
    ).reshape(levels, buffer_len)
    offsets = (0, rows_y, 1, rows_y + 1)
    adjoint = jnp.zeros((levels, rows_x * rows_y), jnp.float32)
    for corner in range(4):
        adjoint = adjoint.at[:, corner_base + offsets[corner]].add(
            weights_flat[corner][None, :] * forcing
        )
    smoothed = diffuse_all(sigma * adjoint.reshape(levels, rows_x, rows_y), face_x, face_y)
    gradient = control + wet_cells[None] * vertical_solve(
        smoothed, lower_diff, upper_factor, inverse
    )
    return (increment, departures, gradient)


def solution(mesh):
    in_specs = (
        P(None, "gx", "gy"),
        P(None, "gx", "gy"),
        P(None, "gx", "gy"),
        P("gx", "gy"),
        P("gx", "gy"),
        P("gx", "gy"),
        P(("gx", "gy"), None),
        P(("gx", "gy")),
        P(None, ("gx", "gy")),
        P(None, ("gx", "gy")),
        P(None, ("gx", "gy")),
    )
    out_specs = (P(None, "gx", "gy"), P(None, ("gx", "gy")), P(None, "gx", "gy"))
    return jax.shard_map(shards, mesh=mesh, in_specs=in_specs, out_specs=out_specs, check_vma=False)
```

profile of v0, /device:TPU:1, one launch (start us, length us, event | category | flops | bytes accessed | tf_op | source)
XLA Modules:
  0.0 1259.4 jit_solution(15495401239803489622)
XLA Ops:
  11.7 34.8 %while.65 = (s32[]{:T(128)}, f32[8,5,1024]{2,1,0:T(8,128)}, s32[2048]{0:T(1024)S(1)}, s32[8]{0:T(128)S(1)}, f32[5,2048]{1,0:T(8,128)S(1)}, /*index=5*/s32[]{:T(128)}) while((s32[]{:T(128)}, f32[8,5,1024]{2,1,0:T(8,128)}, s32[2048]{0:T(1024)S(1)}, s32[8]{0:T(128)S(1)}, f32[5,2048]{1,0:T(8,128)S(1)}, /*index=5*/s32[]{:T(128)}) %tuple.226), condition=%wide.region_6.7_spmd, body=%wide.region_5.6_spmd.sunk | while | flops 127927296 | bytes 90209 | solution.py:112
  48.3 13.8 %all-to-all-start.1 = ((s32[1,128,64]{2,0,1:T(1,128)}), s32[1,128,64]{2,0,1:T(1,128)}, u32[]{:S(2)}, u32[]{:S(2)}) async-start(s32[1,128,64]{2,0,1:T(1,128)} %bitcast.17), calls=%async_computation.1 | async-start | bytes 131072 | tf_op jit(solution)/shard_map/all_to_all | solution.py:192
  76.9 312.6 %while.64 = (s32[]{:T(128)}, f32[16,64,256]{2,0,1:T(8,128)S(1)}, f32[66,258]{1,0:T(8,128)S(1)}, f32[66,258]{1,0:T(8,128)S(1)}, s32[]{:T(128)}) while((s32[]{:T(128)}, f32[16,64,256]{2,0,1:T(8,128)S(1)}, f32[66,258]{1,0:T(8,128)S(1)}, f32[66,258]{1,0:T(8,128)S(1)}, s32[]{:T(128)}) %tuple.220), condition=%wide.region_1.0_spmd, body=%wide.region_0.0_spmd.sunk | while | flops 5247106 | bytes 9029341 | solution.py:68
  187.4 10.6 fusion.155
  344.6 10.6 fusion.155
  396.1 10.7 all-to-all-start
  409.5 31.3 %gather_fusion.3 = f32[8192,16]{1,0:T(8,128)} fusion(f32[16,16384]{0,1:T(8,128)} %bitcast.125, s32[8192]{0:T(1024)S(1)} %get-tuple-element.429), kind=kCustom, calls=%fused_computation.3 | custom fusion | bytes 1081344 | tf_op jit(solution)/shard_map/gather | solution.py:77
  444.7 31.3 %gather_fusion.2 = f32[8192,16]{1,0:T(8,128)} fusion(f32[16,16384]{0,1:T(8,128)} %bitcast.126, s32[8192]{0:T(1024)S(1)} %get-tuple-element.430), kind=kCustom, calls=%fused_computation.2 | custom fusion | bytes 1081344 | tf_op jit(solution)/shard_map/gather | solution.py:77
  480.3 31.3 %gather_fusion.1 = f32[8192,16]{1,0:T(8,128)} fusion(f32[16,16384]{0,1:T(8,128)} %bitcast.127, s32[8192]{0:T(1024)S(1)} %get-tuple-element.431), kind=kCustom, calls=%fused_computation.1 | custom fusion | bytes 1081344 | tf_op jit(solution)/shard_map/gather | solution.py:77
  515.6 31.3 %gather_fusion = f32[8192,16]{1,0:T(8,128)} fusion(f32[16,16384]{0,1:T(8,128)} %bitcast.128, s32[8192]{0:T(1024)S(1)} %get-tuple-element.432), kind=kCustom, calls=%fused_computation | custom fusion | bytes 1081344 | tf_op jit(solution)/shard_map/gather | solution.py:77
  567.4 13.0 %all-to-all-done.2 = f32[128,1,1024]{2,1,0:T(1,128)S(1)} async-done(((f32[128,1,1024]{2,1,0:T(1,128)}), f32[128,1,1024]{2,1,0:T(1,128)S(1)}, u32[]{:S(2)}, u32[]{:S(2)}) %all-to-all-start.2) | async-done | bytes 524320 | tf_op jit(solution)/shard_map/all_to_all | solution.py:198
  583.3 51.9 %while.69 = (s32[]{:T(128)}, f32[16,2048]{1,0:T(8,128)}, f32[8,16,1024]{2,0,1:T(8,128)S(1)}, s32[2048]{0:T(1024)S(1)}, s32[8]{0:T(128)S(1)}, /*index=5*/s32[]{:T(128)}, s32[]{:T(128)}) while((s32[]{:T(128)}, f32[16,2048]{1,0:T(8,128)}, f32[8,16,1024]{2,0,1:T(8,128)S(1)}, s32[2048]{0:T(1024)S(1)}, s32[8]{0:T(128)S(1)}, ...), condition=%wide.region_8.9_spmd.clone, body=%wide.region_7.8_spmd.clone.sunk | while | flops 404816896 | bytes 475251 | solution.py:137
  636.7 30.0 %while.66 = (s32[]{:T(128)}, f32[8,16,1024]{2,1,0:T(8,128)S(1)}, s32[2048]{0:T(1024)S(1)}, s32[8]{0:T(128)S(1)}, f32[16,2048]{1,0:T(8,128)S(1)}, /*index=5*/s32[]{:T(128)}) while((s32[]{:T(128)}, f32[8,16,1024]{2,1,0:T(8,128)S(1)}, s32[2048]{0:T(1024)S(1)}, s32[8]{0:T(128)S(1)}, f32[16,2048]{1,0:T(8,128)S(1)}, /*index=5*/s32[]{:T(128)}) %tuple.244), condition=%wide.region_10.11_spmd, body=%wide.region_9.10_spmd.sunk | while | flops 404751360 | bytes 213089 | solution.py:112
  675.2 12.7 %all-to-all-done.3 = f32[128,1,1024]{2,1,0:T(1,128)S(1)} async-done(((f32[128,1,1024]{2,1,0:T(1,128)}), f32[128,1,1024]{2,1,0:T(1,128)S(1)}, u32[]{:S(2)}, u32[]{:S(2)}) %all-to-all-start.3) | async-done | bytes 524320 | tf_op jit(solution)/shard_map/all_to_all | solution.py:208
  693.7 53.7 %scatter_custom_fusion = f32[16,16384]{0,1:T(8,128)} fusion(s32[8192]{0:T(1024)} %copy-done.45, f32[8192,16]{1,0:T(8,128)} %copy.284, f32[]{:T(128)} %constant.54.clone.1), kind=kCustom, calls=%fused_computation.87 | custom fusion | flops 131072 | bytes 1049088 | tf_op jit(solution)/shard_map/scatter-add | solution.py:214
  755.2 55.4 %scatter_fusion = f32[16,16384]{0,1:T(8,128)} fusion(f32[16,16384]{0,1:T(8,128)} %scatter_custom_fusion, s32[8192]{0:T(1024)S(1)} %bitcast.152, f32[8192,16]{1,0:T(8,128)} %copy.285), kind=kCustom, calls=%fused_computation.5 | custom fusion | flops 131072 | bytes 1605632 | tf_op jit(solution)/shard_map/scatter-add | solution.py:214
  810.6 55.6 %scatter_fusion.1 = f32[16,16384]{0,1:T(8,128)} fusion(f32[16,16384]{0,1:T(8,128)} %scatter_fusion, s32[8192]{0:T(1024)S(1)} %bitcast.150, f32[8192,16]{1,0:T(8,128)} %copy.286), kind=kCustom, calls=%fused_computation.6 | custom fusion | flops 131072 | bytes 1605632 | tf_op jit(solution)/shard_map/scatter-add | solution.py:214
  866.3 55.4 %scatter_fusion.2 = f32[16,16384]{0,1:T(8,128)} fusion(f32[16,16384]{0,1:T(8,128)} %scatter_fusion.1, s32[8192]{0:T(1024)S(1)} %bitcast.148, f32[8192,16]{1,0:T(8,128)} %copy.287), kind=kCustom, calls=%fused_computation.7 | custom fusion | flops 131072 | bytes 1605632 | tf_op jit(solution)/shard_map/scatter-add | solution.py:214
  927.5 327.0 %while.67 = (s32[]{:T(128)}, f32[16,64,256]{2,0,1:T(8,128)S(1)}, f32[66,258]{1,0:T(8,128)S(1)}, f32[66,258]{1,0:T(8,128)S(1)}, s32[]{:T(128)}) while((s32[]{:T(128)}, f32[16,64,256]{2,0,1:T(8,128)S(1)}, f32[66,258]{1,0:T(8,128)S(1)}, f32[66,258]{1,0:T(8,128)S(1)}, s32[]{:T(128)}) %tuple.239), condition=%wide.region_16.17_spmd, body=%wide.region_15.16_spmd.sunk | while | flops 5247106 | bytes 9029341 | solution.py:68
  928.2 13.4 %collective-permute-start.5 = (f32[16,1,256]{2,0,1:T(8,128)S(1)}, f32[16,1,256]{2,0,1:T(8,128)S(1)}, u32[]{:S(2)}, u32[]{:S(2)}) collective-permute-start(f32[16,1,256]{2,0,1:T(8,128)S(1)} %get-tuple-element.619), channel_id=1, source_target_pairs={{0,8},{8,16},{16,24},{24,32},{32,40},{40,48},{48,56},{56,64},{64,7... | collective-permute-start | bytes 49160 | tf_op jit(solution)/shard_map/while/body/eval_jaxpr/ppermute | solution.py:16
  1052.5 10.6 fusion.164
  1115.3 10.6 fusion.164
  1146.7 10.6 fusion.164
  1178.2 10.6 fusion.164
  (722 shorter events, 786.9 us)
Async XLA Ops:
  2.3 62.3 %collective-permute-start.9 = (f32[3,1,256]{2,1,0:T(1,128)S(1)}, f32[3,1,256]{2,1,0:T(1,128)S(1)}, u32[]{:S(2)}, u32[]{:S(2)}) collective-permute-start(f32[3,1,256]{2,1,0:T(1,128)S(1)} %get-tuple-element.424), channel_id=1, source_target_pairs={{8,0},{16,8},{24,16},{32,24},{40,32},{48,40},{56,48},{64,56},{72,6... | collective-permute-start | bytes 9224 | tf_op jit(solution)/shard_map/ppermute | solution.py:17
  3.7 60.9 %collective-permute-start.8 = (f32[3,1,256]{2,1,0:T(1,128)S(1)}, f32[3,1,256]{2,1,0:T(1,128)S(1)}, u32[]{:S(2)}, u32[]{:S(2)}) collective-permute-start(f32[3,1,256]{2,1,0:T(1,128)S(1)} %get-tuple-element.423), channel_id=1, source_target_pairs={{0,8},{8,16},{16,24},{24,32},{32,40},{40,48},{48,56},{56,64},{64,7... | collective-permute-start | bytes 9224 | tf_op jit(solution)/shard_map/ppermute | solution.py:16
  48.3 347.9 %all-to-all-start.1 = ((s32[1,128,64]{2,0,1:T(1,128)}), s32[1,128,64]{2,0,1:T(1,128)}, u32[]{:S(2)}, u32[]{:S(2)}) async-start(s32[1,128,64]{2,0,1:T(1,128)} %bitcast.17), calls=%async_computation.1 | async-start | bytes 131072 | tf_op jit(solution)/shard_map/all_to_all | solution.py:192
  66.0 8.6 collective-permute-start.11
  106.2 8.0 collective-permute-start
  138.8 6.7 collective-permute-start
  201.5 6.8 collective-permute-start
  233.0 6.8 collective-permute-start
  264.4 6.8 collective-permute-start
  295.9 6.8 collective-permute-start
  327.3 6.8 collective-permute-start
  358.7 6.8 collective-permute-start
  396.1 154.7 %all-to-all-start = ((f32[128,1,256]{2,1,0:T(1,128)}), f32[128,1,256]{2,1,0:T(1,128)S(1)}, u32[]{:S(2)}, u32[]{:S(2)}) async-start(f32[128,1,256]{2,1,0:T(1,128)} %reshape.333), calls=%async_computation | async-start | bytes 262144 | tf_op jit(solution)/shard_map/all_to_all | solution.py:193
  557.3 23.1 %all-to-all-start.2 = ((f32[128,1,1024]{2,1,0:T(1,128)}), f32[128,1,1024]{2,1,0:T(1,128)S(1)}, u32[]{:S(2)}, u32[]{:S(2)}) async-start(f32[128,1,1024]{2,1,0:T(1,128)} %reshape.335), calls=%async_computation.2 | async-start | bytes 1048576 | tf_op jit(solution)/shard_map/all_to_all | solution.py:198
  669.4 18.5 %all-to-all-start.3 = ((f32[128,1,1024]{2,1,0:T(1,128)}), f32[128,1,1024]{2,1,0:T(1,128)S(1)}, u32[]{:S(2)}, u32[]{:S(2)}) async-start(f32[128,1,1024]{2,1,0:T(1,128)} %reshape.337), calls=%async_computation.3 | async-start | bytes 1048576 | tf_op jit(solution)/shard_map/all_to_all | solution.py:208
  928.2 15.0 %collective-permute-start.4 = (f32[16,1,256]{2,0,1:T(8,128)}, f32[16,1,256]{2,0,1:T(8,128)S(1)}, u32[]{:S(2)}, u32[]{:S(2)}) collective-permute-start(f32[16,1,256]{2,0,1:T(8,128)} %get-tuple-element.618), channel_id=1, source_target_pairs={{8,0},{16,8},{24,16},{32,24},{40,32},{48,40},{56,48},{64,56},{72,6... | collective-permute-start | bytes 49160 | tf_op jit(solution)/shard_map/while/body/eval_jaxpr/ppermute | solution.py:17
  928.2 17.5 %collective-permute-start.5 = (f32[16,1,256]{2,0,1:T(8,128)S(1)}, f32[16,1,256]{2,0,1:T(8,128)S(1)}, u32[]{:S(2)}, u32[]{:S(2)}) collective-permute-start(f32[16,1,256]{2,0,1:T(8,128)S(1)} %get-tuple-element.619), channel_id=1, source_target_pairs={{0,8},{8,16},{16,24},{24,32},{32,40},{40,48},{48,56},{56,64},{64,7... | collective-permute-start | bytes 49160 | tf_op jit(solution)/shard_map/while/body/eval_jaxpr/ppermute | solution.py:16
  971.8 7.1 collective-permute-start.4
  1003.3 7.3 collective-permute-start.4
  1098.0 6.8 collective-permute-start.4
  1129.4 6.8 collective-permute-start.4
  1160.9 6.8 collective-permute-start.4
  1192.4 6.7 collective-permute-start.4
  1223.7 6.8 collective-permute-start.4
  (114 other events, 666.2 us)
where the time goes:
time: 1270 us; the launch traced here: 1260 us
  other arithmetic  486 us (38%)
  local copies, waits for them, and re-layouts  403 us (32%)
  starting transfers between devices  237 us (19%)
  matrix products  89.8 us (7%)
  waiting for transfers between devices  39.4 us (3%)
    scatter-add x4, other arithmetic, shards(): adjoint.at[:, corner_base + offsets[corner]]  220 us
    sub x20, other arithmetic, stencil(): return centre + east_flux - west_flux + north_flux - south_flux  212 us
    ppermute x42, starting transfers between devices, extended_2(): after = lax.ppermute(initial, axis, down)  176 us
    gather x8, local copies, waits for them, and re-layouts, interpolate(): field_flat[:, corner_base + offsets[corner]]  141 us
    another operation x40, local copies, waits for them, and re-layouts  89.6 us
    ppermute x20, local copies, waits for them, and re-layouts, extended_2(): after = lax.ppermute(initial, axis, down)  48.4 us
    ppermute x20, local copies, waits for them, and re-layouts, extended_2(): before = lax.ppermute(last, axis, up)  47.6 us
    dot_general x16, matrix products, place(): jnp.dot(records, placing, precision=lax.Precision.HIGHEST, preferred_elem...  44.9 us
  transfers between devices with their start and end apart: 88, of which 24 were waited for; matrix products, arithmetic and copies ran while one was open for 37% of the time, Pallas kernels for 0%

commit v1 on v0

v1 whole, which is shorter than its diff:
```python
import functools

import jax
import jax.numpy as jnp
from jax import lax
from jax.experimental import pallas as pl
from jax.experimental.pallas import tpu as pltpu
from jax.sharding import PartitionSpec as P

MESH = pl.DeviceIdType.MESH
F32 = jnp.float32
BF16 = jnp.bfloat16
VMEM_LIMIT = 60 * 1024 * 1024

LEV = 16
STEPS = 10
CX = 64
CY = 256
NGX = 16
NGY = 8
NDEV = NGX * NGY
PROF = 2048
CAP = 64
TILES = PROF // 128
ROWS = CX + 2 * STEPS
SPAD = 6
SROWS = 96
GROUPS = 12
REC = 24
DIFFUSE_ROWS = 16
PACK_PAIRS = 4
UNPACK_OWNERS = 8


def lane_iota(rows):
    return lax.broadcasted_iota(jnp.int32, (rows, 128), 1)


def split_pair(low, high, left):
    first = jnp.where(left, low, pltpu.roll(high, 64, axis=1))
    second = jnp.where(left, pltpu.roll(low, 64, axis=1), high)
    return first, second


def pack_kernel(owner, cell, weights, innov, obsw, rec, rank_out, tab, cst):
    rows_o = lax.broadcasted_iota(jnp.int32, (NDEV, 256), 0)
    before = (
        lax.broadcasted_iota(jnp.int32, (256, 256), 0) < lax.broadcasted_iota(jnp.int32, (256, 256), 1)
    ).astype(F32).astype(BF16)
    ones = jnp.ones((256, 256), BF16)
    rows_r = lax.broadcasted_iota(jnp.int32, (CAP, 256), 0)
    cols_p = lax.broadcasted_iota(jnp.int32, (CAP, 256), 1)
    earlier = jnp.zeros((NDEV, 256), F32)
    table = jnp.zeros((NDEV, 128), F32)
    for block in range(PROF // 256):
        owners = jnp.concatenate([owner[2 * block : 2 * block + 1, :], owner[2 * block + 1 : 2 * block + 2, :]], axis=1)
        hot = (rows_o == owners).astype(F32)
        hot16 = hot.astype(BF16)
        count = earlier + jnp.dot(hot16, before, preferred_element_type=F32)
        rank = jnp.sum(hot * count, axis=0, keepdims=True).astype(jnp.int32)
        earlier = earlier + jnp.dot(hot16, ones, preferred_element_type=F32)
        rank_out[2 * block : 2 * block + 1, :] = rank[:, :128]
        rank_out[2 * block + 1 : 2 * block + 2, :] = rank[:, 128:]
        same = rows_r == rank
        lane = jnp.where(same, cols_p % 128, 0).astype(F32).astype(BF16)
        tile = jnp.where(same, 2 * block + 1 + cols_p // 128, 0).astype(F32).astype(BF16)
        table = table + lax.dot_general(
            hot16, jnp.concatenate([lane, tile], axis=0), (((1,), (1,)), ((), ())), preferred_element_type=F32
        )
    tab[...] = table.astype(jnp.int32)

    cst[...] = jnp.zeros_like(cst)
    for tile in range(TILES):
        cols = slice(128 * tile, 128 * tile + 128)
        cst[0:1, cols] = cell[tile : tile + 1, :].astype(F32)
        cst[1:2, cols] = weights[1:2, cols] + weights[3:4, cols]
        cst[2:3, cols] = weights[2:3, cols] + weights[3:4, cols]

    left = lane_iota(8) < 64

    def pair(j, carry):
        row0 = jnp.broadcast_to(tab[pl.ds(2 * j, 1), :], (8, 128))
        row1 = jnp.broadcast_to(tab[pl.ds(2 * j + 1, 1), :], (8, 128))
        lane = jnp.where(left, row0, pltpu.roll(row1, 64, axis=1))
        tile_of = jnp.where(left, pltpu.roll(row0, 64, axis=1), row1)
        found = [jnp.zeros((8, 128), F32)] * 5
        for tile in range(TILES):
            cols = slice(128 * tile, 128 * tile + 128)
            sources = (cst[:, cols], innov[0:8, cols], innov[8:16, cols], obsw[0:8, cols], obsw[8:16, cols])
            here = tile_of == tile + 1
            found = [
                jnp.where(here, jnp.take_along_axis(source, lane, axis=1, mode="promise_in_bounds"), old)
                for source, old in zip(sources, found)
            ]
        first_i, second_i = split_pair(found[1], found[2], left)
        first_o, second_o = split_pair(found[3], found[4], left)
        rec[2 * j] = jnp.concatenate([found[0], first_i, first_o], axis=0)
        rec[2 * j + 1] = jnp.concatenate([pltpu.roll(found[0], 64, axis=1), second_i, second_o], axis=0)
        return carry

    blocks(0, NDEV // 2, PACK_PAIRS, pair, 0)


def pack(owner, cell, weights, innov, obsw):
    return pl.pallas_call(
        pack_kernel,
        out_shape=(
            jax.ShapeDtypeStruct((NDEV, REC, 128), F32),
            jax.ShapeDtypeStruct((TILES, 128), jnp.int32),
        ),
        in_specs=[pl.BlockSpec(memory_space=pltpu.VMEM)] * 5,
        out_specs=(pl.BlockSpec(memory_space=pltpu.VMEM),) * 2,
        scratch_shapes=[pltpu.VMEM((NDEV, 128), jnp.int32), pltpu.VMEM((8, PROF), F32)],
        compiler_params=pltpu.CompilerParams(vmem_limit_bytes=VMEM_LIMIT),
        name="pack",
    )(owner, cell, weights, innov, obsw)


def unpack_kernel(ret, owner, rank, innov, dep):
    def one(o, found):
        tile = ret[o]
        new = []
        for t in range(TILES):
            idx = jnp.broadcast_to(rank[t : t + 1, :], (8, 128))
            here = jnp.broadcast_to(owner[t : t + 1, :], (8, 128)) == o
            low = jnp.take_along_axis(tile, idx, axis=1, mode="promise_in_bounds")
            high = jnp.take_along_axis(tile, idx + 64, axis=1, mode="promise_in_bounds")
            new.append(jnp.where(here, low, found[2 * t]))
            new.append(jnp.where(here, high, found[2 * t + 1]))
        return tuple(new)

    found = blocks(0, NDEV, UNPACK_OWNERS, one, tuple(jnp.zeros((8, 128), F32) for _ in range(2 * TILES)))
    for t in range(TILES):
        cols = slice(128 * t, 128 * t + 128)
        dep[0:8, cols] = found[2 * t] - innov[0:8, cols]
        dep[8:16, cols] = found[2 * t + 1] - innov[8:16, cols]


def unpack(ret, owner, rank, innov):
    return pl.pallas_call(
        unpack_kernel,
        out_shape=jax.ShapeDtypeStruct((LEV, PROF), F32),
        in_specs=[pl.BlockSpec(memory_space=pltpu.VMEM)] * 4,
        out_specs=pl.BlockSpec(memory_space=pltpu.VMEM),
        compiler_params=pltpu.CompilerParams(vmem_limit_bytes=VMEM_LIMIT),
        name="unpack",
    )(ret, owner, rank, innov)


def pack_sides(main, low_side, high_side, lev):
    slot = lane_iota(lev) // 16

    def group(g, carry):
        low = jnp.zeros((lev, 128), F32)
        high = jnp.zeros((lev, 128), F32)
        for m in range(8):
            at = pl.ds(pl.multiple_of((STEPS + 8 * g + m) * lev, lev), lev)
            here = slot == m
            first = main[0, at, :]
            last = main[1, at, :]
            low = jnp.where(here, first if m == 0 else pltpu.roll(first, 16 * m, axis=1), low)
            high = jnp.where(here, last if m == 7 else pltpu.roll(last, 16 * m + 16, axis=1), high)
        at = pl.ds(pl.multiple_of(g * lev, lev), lev)
        low_side[at, :] = low
        high_side[at, :] = high
        return carry

    lax.fori_loop(0, CX // 8, group, 0)


def unpack_sides(from_high, from_low, side, lev):
    left = lane_iota(lev) < 64

    def group(g, carry):
        at = pl.ds(pl.multiple_of(g * lev, lev), lev)
        right_strip = from_high[at, :]
        left_strip = from_low[at, :]
        for m in range(8):
            right = right_strip if m == 0 else pltpu.roll(right_strip, 128 - 16 * m, axis=1)
            leftv = left_strip if m == 7 else pltpu.roll(left_strip, 112 - 16 * m, axis=1)
            side[pl.ds(pl.multiple_of((8 * g + m) * lev, lev), lev), :] = jnp.where(left, right, leftv)
        return carry

    lax.fori_loop(0, GROUPS, group, 0)


def halo_copies(main, low_side, high_side, from_high, from_low, send_sem, recv_sem, gx, gy, lev):
    west, east = (gx + NGX - 1) % NGX, (gx + 1) % NGX
    south, north = (gy + NGY - 1) % NGY, (gy + 1) % NGY

    def rows(ref, start, count):
        at = pl.ds(start * lev, count * lev)
        return ref.at[:, at, :] if len(ref.shape) == 3 else ref.at[at, :]

    plan = (
        (rows(main, STEPS, STEPS), rows(main, STEPS + CX, STEPS), (west, gy)),
        (rows(main, CX, STEPS), rows(main, 0, STEPS), (east, gy)),
        (rows(low_side, 0, 8), rows(from_high, 2, 8), (gx, south)),
        (rows(high_side, 0, 8), rows(from_low, 2, 8), (gx, north)),
        (rows(low_side, 0, 2), rows(from_high, 10, 2), (west, south)),
        (rows(low_side, 6, 2), rows(from_high, 0, 2), (east, south)),
        (rows(high_side, 0, 2), rows(from_low, 10, 2), (west, north)),
        (rows(high_side, 6, 2), rows(from_low, 0, 2), (east, north)),
    )
    return [
        pltpu.make_async_remote_copy(
            src_ref=src,
            dst_ref=dst,
            send_sem=send_sem.at[i],
            recv_sem=recv_sem.at[i],
            device_id=device,
            device_id_type=MESH,
        )
        for i, (src, dst, device) in enumerate(plan)
    ]


def next_cols(parts, last):
    rolled = [pltpu.roll(part, 127, axis=1) for part in parts]
    return [jnp.where(last, rolled[(i + 1) % 3], rolled[i]) for i in range(3)]


def prev_cols(parts, first):
    rolled = [pltpu.roll(part, 1, axis=1) for part in parts]
    return [jnp.where(first, rolled[(i + 2) % 3], rolled[i]) for i in range(3)]


def blocks(start, count, width, body, carry):
    def many(i, carry):
        for q in range(width):
            carry = body(start + width * i + q, carry)
        return carry

    carry = lax.fori_loop(0, count // width, many, carry)
    for q in range(count - count % width, count):
        carry = body(start + q, carry)
    return carry


def build_faces(coef, coef_side, gy):
    lane = lane_iota(1)
    first_part = jnp.where(gy < NGY - 1, 1.0, 0.0).astype(F32)
    last_part = jnp.where(gy > 0, 1.0, 0.0).astype(F32)
    inside = jnp.where(lane < 64, first_part, last_part)
    last, first = lane == 127, lane == 0

    def row(r, which):
        at = pl.ds(r * 8 + which, 1)
        return [coef[0, at, :], coef[1, at, :], coef_side[pl.ds((r + SPAD) * 8 + which, 1), :]]

    def put(r, which, parts):
        at = pl.ds(r * 8 + which, 1)
        coef[0, at, :] = parts[0]
        coef[1, at, :] = parts[1]
        coef_side[pl.ds((r + SPAD) * 8 + which, 1), :] = parts[2]

    def wet_row(r):
        one, two, side = row(r, 2)
        return [one, two, side * inside]

    def one(r, wet):
        ahead = wet_row(r + 1)
        zonal, merid = row(r, 0), row(r, 1)
        north = next_cols(wet, last)
        south = prev_cols(wet, first)
        merid_south = prev_cols(merid, first)
        put(r, 0, [z * w * a for z, w, a in zip(zonal, wet, ahead)])
        put(r, 1, [m * w * n for m, w, n in zip(merid, wet, north)])
        put(r, 3, [m * w * n for m, w, n in zip(merid_south, south, wet)])
        return tuple(ahead)

    blocks(0, ROWS - 1, 8, one, tuple(wet_row(0)))


def diffuse(first_main, first_side, second_main, second_side, coef, coef_side):
    lane = lane_iota(LEV)
    last, first = lane == 127, lane == 0

    def face(r, which):
        at = pl.ds(r * 8 + which, 1)
        parts = [coef[0, at, :], coef[1, at, :], coef_side[pl.ds((r + SPAD) * 8 + which, 1), :]]
        return [jnp.broadcast_to(part, (LEV, 128)) for part in parts]

    for step in range(STEPS):
        even = step % 2 == 0
        main, side = (first_main, first_side) if even else (second_main, second_side)
        new_main, new_side = (second_main, second_side) if even else (first_main, first_side)
        final = step == STEPS - 1

        def field(r):
            at = pl.ds(pl.multiple_of(r * LEV, LEV), LEV)
            return [main[0, at, :], main[1, at, :], side[pl.ds(pl.multiple_of((r + SPAD) * LEV, LEV), LEV), :]]

        def flux(r, here, ahead):
            return [f * (a - h) for f, a, h in zip(face(r, 0), ahead, here)]

        def one(r, carry):
            here, behind = carry[:3], carry[3:]
            ahead = field(r + 1)
            east = flux(r, here, ahead)
            north = [f * (n - h) for f, n, h in zip(face(r, 1), next_cols(here, last), here)]
            south = [f * (h - p) for f, p, h in zip(face(r, 3), prev_cols(here, first), here)]
            new = [h + ((e - w) + (n - s)) for h, e, w, n, s in zip(here, east, behind, north, south)]
            at = pl.ds(pl.multiple_of(r * LEV, LEV), LEV)
            new_main[0, at, :] = new[0]
            new_main[1, at, :] = new[1]
            if not final:
                new_side[pl.ds(pl.multiple_of((r + SPAD) * LEV, LEV), LEV), :] = new[2]
            return tuple(ahead) + tuple(east)

        start = step + 1
        here = field(start)
        behind = flux(start - 1, field(start - 1), here)
        blocks(start, ROWS - 2 * start, DIFFUSE_ROWS, one, tuple(here) + tuple(behind))


SOLVE_ROWS = 32


def load_level(ref, level, x, lev, count):
    at = pl.ds((STEPS + x) * lev + level, count, stride=lev)
    return jnp.concatenate([ref[0, at, :], ref[1, at, :]], axis=1)


def store_level(ref, level, x, lev, count, value):
    at = pl.ds((STEPS + x) * lev + level, count, stride=lev)
    ref[0, at, :] = value[:, 0:128]
    ref[1, at, :] = value[:, 128:256]


def solve_first(control, vert, mask, upper, inverse, reduced, main):
    for x in range(0, CX, SOLVE_ROWS):
        rows = slice(x, x + SOLVE_ROWS)
        wet = mask[rows, :].astype(F32)
        previous = None
        for k in range(LEV):
            rhs = wet * control[k, rows, :]
            diagonal = 1.0
            if k > 0:
                below = vert[k - 1, rows, :]
                diagonal = diagonal + below
            if k < LEV - 1:
                above = vert[k, rows, :]
                diagonal = diagonal + above
            if k > 0:
                diagonal = diagonal + below * up
                rhs = rhs + below * previous
            inv = 1.0 / diagonal
            inverse[k, rows, :] = inv
            if k < LEV - 1:
                up = -above * inv
                upper[k, rows, :] = up
            previous = rhs * inv
            if k < LEV - 1:
                reduced[k, rows, :] = previous
        value = previous
        store_level(main, LEV - 1, x, LEV, SOLVE_ROWS, value)
        for k in range(LEV - 2, -1, -1):
            value = reduced[k, rows, :] - upper[k, rows, :] * value
            store_level(main, k, x, LEV, SOLVE_ROWS, value)


def solve_last(main, control, vert, mask, upper, inverse, reduced, grad):
    for x in range(0, CX, SOLVE_ROWS):
        rows = slice(x, x + SOLVE_ROWS)
        wet = mask[rows, :].astype(F32)
        previous = None
        for k in range(LEV):
            rhs = load_level(main, k, x, LEV, SOLVE_ROWS)
            if k > 0:
                rhs = rhs + vert[k - 1, rows, :] * previous
            previous = rhs * inverse[k, rows, :]
            if k < LEV - 1:
                reduced[k, rows, :] = previous
        value = previous
        grad[LEV - 1, rows, :] = control[LEV - 1, rows, :] + wet * value
        for k in range(LEV - 2, -1, -1):
            value = reduced[k, rows, :] - upper[k, rows, :] * value
            grad[k, rows, :] = control[k, rows, :] + wet * value


def observe_all(recv, field3, adj, ret_send):
    left = lane_iota(8) < 64
    rows_b = lax.broadcasted_iota(jnp.int32, (CY, 256), 0).astype(F32)
    rows_a = lax.broadcasted_iota(jnp.int32, (CX, 256), 0).astype(F32)

    def observe(i, carry):
        pairs = []
        for h in range(2):
            one, two = recv[4 * i + 2 * h], recv[4 * i + 2 * h + 1]
            place = jnp.where(left, one[0:8], pltpu.roll(two[0:8], 64, axis=1))
            low_i = jnp.where(left, one[8:16], pltpu.roll(two[8:16], 64, axis=1))
            high_i = jnp.where(left, pltpu.roll(one[8:16], 64, axis=1), two[8:16])
            low_o = jnp.where(left, one[16:24], pltpu.roll(two[16:24], 64, axis=1))
            high_o = jnp.where(left, pltpu.roll(one[16:24], 64, axis=1), two[16:24])
            pairs.append((place, jnp.concatenate([low_i, high_i], axis=0), jnp.concatenate([low_o, high_o], axis=0)))
        place, innov, obsw = [jnp.concatenate([pairs[0][n], pairs[1][n]], axis=1) for n in range(3)]
        cell, along_x, along_y = place[0:1], place[1:2], place[2:3]
        cell_a = jnp.floor(cell * (1.0 / CY))
        cell_b = cell - CY * cell_a
        from_a = rows_a - cell_a
        from_b = rows_b - cell_b
        in_x = jnp.where(from_a == 0.0, 1.0 - along_x, jnp.where(from_a == 1.0, along_x, 0.0))
        in_y = jnp.where(from_b == 0.0, 1.0 - along_y, jnp.where(from_b == 1.0, along_y, 0.0))
        y_high = in_y.astype(BF16)
        y_low = (in_y - y_high.astype(F32)).astype(BF16)
        rows = jnp.dot(
            field3[...], jnp.concatenate([y_high, y_low, y_high], axis=0), preferred_element_type=F32
        )
        vals = jnp.sum(rows.reshape(LEV, CX, 256) * in_x[None], axis=1)
        forcing = obsw * (vals - innov)
        for h in range(2):
            cols = slice(128 * h, 128 * h + 128)
            first, second = split_pair(vals[0:8, cols], vals[8:16, cols], left)
            ret_send[4 * i + 2 * h] = first
            ret_send[4 * i + 2 * h + 1] = second
        spread = (in_x[None] * forcing[:, None, :]).reshape(LEV * CX, 256)
        high = spread.astype(BF16)
        low = (spread - high.astype(F32)).astype(BF16)
        adj[...] += lax.dot_general(
            jnp.concatenate([high, high, low], axis=1),
            jnp.concatenate([y_high, y_low, y_high], axis=1),
            (((1,), (1,)), ((), ())),
            preferred_element_type=F32,
        )
        return carry

    lax.fori_loop(0, NDEV // 4, observe, 0)


def main_kernel(
    control, sigma, vert, zonal, merid, mask, rec, inc, ret, grad,
    recv, ret_send, coef, coef_side, coef_low, coef_high, coef_from_high, coef_from_low,
    main_a, side_a, main_b, side_b, main_c, side_c,
    low_a, high_a, from_high_a, from_low_a, low_c, high_c, from_high_c, from_low_c,
    upper, inverse, reduced, field3, adj,
    rec_send_sem, rec_recv_sem, ret_send_sem, ret_recv_sem, self_sem, halo_send, halo_recv,
):
    gx, gy = lax.axis_index("gx"), lax.axis_index("gy")
    me = gx * NGY + gy

    barrier = pltpu.get_barrier_semaphore()

    def greet(d, carry):
        to = (me + d) % NDEV
        pl.semaphore_signal(barrier, inc=1, device_id=(to // NGY, to % NGY), device_id_type=MESH)
        return carry

    lax.fori_loop(1, NDEV, greet, 0)
    pl.semaphore_wait(barrier, NDEV - 1)

    def rec_copy(to):
        return pltpu.make_async_remote_copy(
            src_ref=rec.at[to], dst_ref=recv.at[me], send_sem=rec_send_sem, recv_sem=rec_recv_sem,
            device_id=(to // NGY, to % NGY), device_id_type=MESH,
        )

    def ret_copy(to):
        return pltpu.make_async_remote_copy(
            src_ref=ret_send.at[to], dst_ref=ret.at[me], send_sem=ret_send_sem, recv_sem=ret_recv_sem,
            device_id=(to // NGY, to % NGY), device_id_type=MESH,
        )

    for half in range(2):
        coef[half, STEPS * 8 : (STEPS + CX) * 8, :] = jnp.zeros((CX * 8, 128), F32)
    for x in range(0, CX, SOLVE_ROWS):
        rows = slice(x, x + SOLVE_ROWS)
        store_level(coef, 0, x, 8, SOLVE_ROWS, zonal[rows, :])
        store_level(coef, 1, x, 8, SOLVE_ROWS, merid[rows, :])
        store_level(coef, 2, x, 8, SOLVE_ROWS, mask[rows, :].astype(F32))
    pack_sides(coef, coef_low, coef_high, 8)
    coef_copies = halo_copies(
        coef, coef_low, coef_high, coef_from_high, coef_from_low, halo_send.at[0], halo_recv.at[0], gx, gy, 8
    )
    for copy in coef_copies:
        copy.start()

    solve_first(control, vert, mask, upper, inverse, reduced, main_a)
    pack_sides(main_a, low_a, high_a, LEV)
    field_copies = halo_copies(
        main_a, low_a, high_a, from_high_a, from_low_a, halo_send.at[1], halo_recv.at[1], gx, gy, LEV
    )
    for copy in field_copies:
        copy.start()

    def send_rec(d, carry):
        rec_copy((me + d) % NDEV).start()
        return carry

    lax.fori_loop(1, NDEV, send_rec, 0)
    own = pltpu.make_async_copy(rec.at[me], recv.at[me], self_sem)
    own.start()

    for copy in coef_copies:
        copy.wait()
    unpack_sides(coef_from_high, coef_from_low, coef_side, 8)
    build_faces(coef, coef_side, gy)
    for copy in field_copies:
        copy.wait()
    unpack_sides(from_high_a, from_low_a, side_a, LEV)
    diffuse(main_a, side_a, main_b, side_b, coef, coef_side)

    def scale(k, carry):
        for x in range(0, CX, 16):
            value = sigma[k, x : x + 16, :] * load_level(main_a, k, x, LEV, 16)
            inc[k, x : x + 16, :] = value
            high = value.astype(BF16)
            low = (value - high.astype(F32)).astype(BF16)
            at = pl.ds(pl.multiple_of(k * CX + x, 16), 16)
            field3[at, 0:256] = high
            field3[at, 256:512] = high
            field3[at, 512:768] = low
        return carry

    lax.fori_loop(0, LEV, scale, 0)

    own.wait()
    whole = pltpu.make_async_remote_copy(
        src_ref=rec.at[pl.ds(0, NDEV - 1)], dst_ref=recv.at[pl.ds(0, NDEV - 1)],
        send_sem=rec_send_sem, recv_sem=rec_recv_sem, device_id=(gx, gy), device_id_type=MESH,
    )
    whole.wait_recv()
    whole.wait_send()

    adj[...] = jnp.zeros_like(adj)
    observe_all(recv, field3, adj, ret_send)

    def weigh(k, carry):
        for x in range(0, CX, SOLVE_ROWS):
            at = pl.ds(pl.multiple_of(k * CX + x, SOLVE_ROWS), SOLVE_ROWS)
            store_level(main_c, k, x, LEV, SOLVE_ROWS, sigma[k, x : x + SOLVE_ROWS, :] * adj[at, :])
        return carry

    lax.fori_loop(0, LEV, weigh, 0)
    pack_sides(main_c, low_c, high_c, LEV)
    adj_copies = halo_copies(
        main_c, low_c, high_c, from_high_c, from_low_c, halo_send.at[2], halo_recv.at[2], gx, gy, LEV
    )
    for copy in adj_copies:
        copy.start()

    def send_ret(d, carry):
        ret_copy((me + d) % NDEV).start()
        return carry

    lax.fori_loop(1, NDEV, send_ret, 0)
    own = pltpu.make_async_copy(ret_send.at[me], ret.at[me], self_sem)
    own.start()

    for copy in adj_copies:
        copy.wait()
    unpack_sides(from_high_c, from_low_c, side_c, LEV)
    diffuse(main_c, side_c, main_b, side_b, coef, coef_side)
    solve_last(main_c, control, vert, mask, upper, inverse, reduced, grad)

    own.wait()
    whole = pltpu.make_async_remote_copy(
        src_ref=ret_send.at[pl.ds(0, NDEV - 1)], dst_ref=ret.at[pl.ds(0, NDEV - 1)],
        send_sem=ret_send_sem, recv_sem=ret_recv_sem, device_id=(gx, gy), device_id_type=MESH,
    )
    whole.wait_recv()
    whole.wait_send()


def gradient_call(control, sigma, vert, zonal, merid, mask, rec):
    vmem = pl.BlockSpec(memory_space=pltpu.VMEM)

    def field(rows, lanes, lev=LEV):
        shape = (rows * lev, 128)
        return pltpu.VMEM(shape if lanes == 128 else (2,) + shape, F32)

    def sides(lev):
        return [field(8, 128, lev), field(8, 128, lev), field(GROUPS, 128, lev), field(GROUPS, 128, lev)]

    return pl.pallas_call(
        main_kernel,
        out_shape=(
            jax.ShapeDtypeStruct((LEV, CX, CY), F32),
            jax.ShapeDtypeStruct((NDEV, 8, 128), F32),
            jax.ShapeDtypeStruct((LEV, CX, CY), F32),
        ),
        in_specs=[vmem] * 7,
        out_specs=(vmem,) * 3,
        scratch_shapes=[
            pltpu.VMEM((NDEV, REC, 128), F32),
            pltpu.VMEM((NDEV, 8, 128), F32),
            field(ROWS, 256, 8), field(SROWS, 128, 8), *sides(8),
            field(ROWS, 256), field(SROWS, 128),
            field(ROWS, 256), field(SROWS, 128),
            field(ROWS, 256), field(SROWS, 128),
            *sides(LEV), *sides(LEV),
            pltpu.VMEM((LEV, CX, CY), F32),
            pltpu.VMEM((LEV, CX, CY), F32),
            pltpu.VMEM((LEV, CX, CY), F32),
            pltpu.VMEM((LEV * CX, 3 * CY), BF16),
            pltpu.VMEM((LEV * CX, CY), F32),
            pltpu.SemaphoreType.DMA, pltpu.SemaphoreType.DMA, pltpu.SemaphoreType.DMA, pltpu.SemaphoreType.DMA,
            pltpu.SemaphoreType.DMA,
            pltpu.SemaphoreType.DMA((3, 8)), pltpu.SemaphoreType.DMA((3, 8)),
        ],
        compiler_params=pltpu.CompilerParams(
            collective_id=0, has_side_effects=True, vmem_limit_bytes=VMEM_LIMIT
        ),
        name="gradient",
    )(control, sigma, vert, zonal, merid, mask, rec)


def shards(control, sigma, vert_diff, zonal_diff, merid_diff, ocean_mask, owner, cell, interp_weights, innovation, obs_weight):
    owner_rows = owner.reshape(TILES, 128)
    cell_rows = cell.reshape(TILES, 128)
    rec, rank = pack(owner_rows, cell_rows, interp_weights, innovation, obs_weight)
    increment, ret, gradient = gradient_call(
        control, sigma, vert_diff, zonal_diff, merid_diff, ocean_mask, rec
    )
    departures = unpack(ret, owner_rows, rank, innovation)
    return increment, departures, gradient


def solution(mesh):
    in_specs = (
        P(None, "gx", "gy"),
        P(None, "gx", "gy"),
        P(None, "gx", "gy"),
        P("gx", "gy"),
        P("gx", "gy"),
        P("gx", "gy"),
        P(("gx", "gy"), None),
        P(("gx", "gy")),
        P(None, ("gx", "gy")),
        P(None, ("gx", "gy")),
        P(None, ("gx", "gy")),
    )
    out_specs = (P(None, "gx", "gy"), P(None, ("gx", "gy")), P(None, "gx", "gy"))
    return jax.shard_map(shards, mesh=mesh, in_specs=in_specs, out_specs=out_specs, check_vma=False)
```

time: 1270 us -> 177 us (0.14)
  other arithmetic: 486 us -> 0 us
  local copies, waits for them, and re-layouts: 403 us -> 3.27 us
  starting transfers between devices: 237 us -> 0 us
  Pallas kernels: 0 us -> 173 us
  matrix products: 89.8 us -> 0 us
  waiting for transfers between devices: 39.4 us -> 0 us
    scatter-add x4 -> x0, other arithmetic: 220 us -> none  [shards(): adjoint.at[:, corner_base + offsets[corner]]]
    sub x20 -> x0, other arithmetic: 212 us -> none  [stencil(): return centre + east_flux - west_flux + north_flux - south_flux]
    ppermute x84 -> x0, starting transfers between devices: 197 us -> none  [the longest x42 176 us: extended_2(): after = lax.ppermute(initial, axis, down)]
    pallas_call x0 -> x3, Pallas kernels: none -> 173 us  [the longest x1 140 us: gradient_call(): pl.pallas_call(main_kernel, out_shape=(jax.ShapeDtypeStruct((LEV, CX, CY)...]
    gather x8 -> x0, local copies, waits for them, and re-layouts: 141 us -> none  [interpolate(): field_flat[:, corner_base + offsets[corner]]]
    ppermute x40 -> x0, local copies, waits for them, and re-layouts: 96 us -> none  [the longest x20 48.4 us: extended_2(): after = lax.ppermute(initial, axis, down)]
    another operation x43 -> x0, local copies, waits for them, and re-layouts: 90.8 us -> none
    dot_general x28 -> x0, matrix products: 89.8 us -> none  [the longest x16 44.9 us: place(): jnp.dot(records, placing, precision=lax.Precision.HIGHEST, preferred_elem...]
  transfers between devices with their start and end apart: 88 -> 0, of which waited for: 24 -> 0; matrix products, arithmetic and copies ran while one was open for 37% -> 0% of each run, Pallas kernels for 0% -> 0%
where the time goes in v1:
time: 177 us
  Pallas kernels  173 us (98%)
  local copies, waits for them, and re-layouts  3.27 us (2%)
    pallas_call x1, Pallas kernels, gradient_call(): pl.pallas_call(main_kernel, out_shape=(jax.ShapeDtypeStruct((LEV, CX, CY)...  140 us
    pallas_call x1, Pallas kernels, pack(): pl.pallas_call(pack_kernel, out_shape=(jax.ShapeDtypeStruct((NDEV, REC, 1...  17.7 us
    pallas_call x1, Pallas kernels, unpack(): pl.pallas_call(unpack_kernel, out_shape=jax.ShapeDtypeStruct((LEV, PROF),...  14.4 us

profile of v1, /device:TPU:1, one launch (start us, length us, event | category | flops | bytes accessed | tf_op | source)
XLA Modules:
  0.0 176.5 jit_solution(2452464820347229862)
XLA Ops:
  0.6 17.7 %pack.1 = (f32[128,24,128]{2,1,0:T(8,128)}, s32[16,128]{1,0:T(8,128)}) custom-call(s32[16,128]{1,0:T(8,128)} %bitcast.2, s32[16,128]{1,0:T(8,128)} %bitcast.4, f32[4,2048]{1,0:T(4,128)} %weights.1, f32[16,2048]{1,0:T(8,128)} %innov.3, f32[16,2048]{1,0:T(8,128)} %obsw.1), custom_call_target="tpu_custom_call" | custom-call | tf_op jit(solution)/shard_map/pack/pallas_call | solution.py:105
  18.3 140.5 %gradient.1 = (f32[16,64,256]{2,1,0:T(8,128)}, f32[128,8,128]{2,1,0:T(8,128)}, f32[16,64,256]{2,1,0:T(8,128)}) custom-call(f32[16,64,256]{2,1,0:T(8,128)} %control.1, f32[16,64,256]{2,1,0:T(8,128)} %sigma.1, f32[15,64,256]{2,1,0:T(8,128)} %vert.1, f32[64,256]{1,0:T(8,128)} %zonal.1, f32[64,256]{1,0:T(8,128)} %merid.1, s32[64,256]{1,0:T(8,128)} %mask.1, ...), custom_call_target="tpu_custom_call" | custom-call | tf_op jit(solution)/shard_map/gradient/pallas_call | solution.py:575
  158.8 0.0 copy-start
  158.9 14.4 %unpack.1 = f32[16,2048]{1,0:T(8,128)} custom-call(f32[128,8,128]{2,1,0:T(8,128)} %get-tuple-element.10.ret, s32[16,128]{1,0:T(8,128)} %bitcast.3, s32[16,128]{1,0:T(8,128)} %get-tuple-element.11.rank, f32[16,2048]{1,0:T(8,128)} %innov.3), custom_call_target="tpu_custom_call" | custom-call | tf_op jit(solution)/shard_map/unpack/pallas_call | solution.py:140
  173.3 2.3 %copy.16 = f32[16,64,256]{2,1,0:T(8,128)} copy(f32[16,64,256]{2,1,0:T(8,128)} %get-tuple-element.16) | data formatting | bytes 2097152
  175.6 0.0 copy-done
  175.6 1.0 copy.17
Async XLA Ops:
  158.8 16.7 %copy-start = (f32[16,64,256]{2,1,0:T(8,128)S(1)}, f32[16,64,256]{2,1,0:T(8,128)}, u32[]{:S(2)}) copy-start(f32[16,64,256]{2,1,0:T(8,128)} %get-tuple-element.18) | copy-start | bytes 3145732

commit v2 on v1

--- a/solution.py
+++ b/solution.py
@@ -26,14 +26,31 @@
 SPAD = 6
 SROWS = 96
 GROUPS = 12
-REC = 24
+REC = 18
 DIFFUSE_ROWS = 16
-PACK_PAIRS = 4
-UNPACK_OWNERS = 8
+PACK_PAIRS = 8
+OBSERVE_TILES = 8
+UNPACK_TILES = 2
 
 
 def lane_iota(rows):
     return lax.broadcasted_iota(jnp.int32, (rows, 128), 1)
+
+
+def blocks(start, count, width, body, carry):
+    def many(i, carry):
+        for q in range(width):
+            carry = body(start + width * i + q, carry)
+        return carry
+
+    carry = lax.fori_loop(0, count // width, many, carry)
+    for q in range(count - count % width, count):
+        carry = body(start + q, carry)
+    return carry
+
+
+def lane_gather(source, lane):
+    return jnp.take_along_axis(source, lane, axis=1, mode="promise_in_bounds")
 
 
 def split_pair(low, high, left):
@@ -42,7 +59,7 @@
     return first, second
 
 
-def pack_kernel(owner, cell, weights, innov, obsw, rec, rank_out, tab, cst):
+def pack_kernel(owner, cell, weights, innov, obsw, rec, rank_out, tab, lanes, tiles, cst, found_ref):
     rows_o = lax.broadcasted_iota(jnp.int32, (NDEV, 256), 0)
     before = (
         lax.broadcasted_iota(jnp.int32, (256, 256), 0) < lax.broadcasted_iota(jnp.int32, (256, 256), 1)
@@ -68,37 +85,60 @@
             hot16, jnp.concatenate([lane, tile], axis=0), (((1,), (1,)), ((), ())), preferred_element_type=F32
         )
     tab[...] = table.astype(jnp.int32)
+    half = lane_iota(NDEV // 2) < 64
+    even, odd = tab[pl.ds(0, NDEV // 2, stride=2), :], tab[pl.ds(1, NDEV // 2, stride=2), :]
+    lanes[...] = jnp.where(half, even, pltpu.roll(odd, 64, axis=1))
+    tiles[...] = jnp.where(half, pltpu.roll(even, 64, axis=1), odd)
 
     cst[...] = jnp.zeros_like(cst)
     for tile in range(TILES):
         cols = slice(128 * tile, 128 * tile + 128)
-        cst[0:1, cols] = cell[tile : tile + 1, :].astype(F32)
-        cst[1:2, cols] = weights[1:2, cols] + weights[3:4, cols]
-        cst[2:3, cols] = weights[2:3, cols] + weights[3:4, cols]
+        to = slice(128 * (tile // 2), 128 * (tile // 2) + 128)
+        row = 4 * (tile % 2)
+        cst[row : row + 1, to] = cell[tile : tile + 1, :].astype(F32)
+        cst[row + 1 : row + 2, to] = weights[1:2, cols] + weights[3:4, cols]
+        cst[row + 2 : row + 3, to] = weights[2:3, cols] + weights[3:4, cols]
 
     left = lane_iota(8) < 64
+    left_row = lane_iota(1) < 64
+    below = lax.broadcasted_iota(jnp.int32, (8, 128), 0) // 4
 
     def pair(j, carry):
-        row0 = jnp.broadcast_to(tab[pl.ds(2 * j, 1), :], (8, 128))
-        row1 = jnp.broadcast_to(tab[pl.ds(2 * j + 1, 1), :], (8, 128))
-        lane = jnp.where(left, row0, pltpu.roll(row1, 64, axis=1))
-        tile_of = jnp.where(left, pltpu.roll(row0, 64, axis=1), row1)
-        found = [jnp.zeros((8, 128), F32)] * 5
+        lane = jnp.broadcast_to(lanes[pl.ds(j, 1), :], (8, 128))
+        tile_of = jnp.broadcast_to(tiles[pl.ds(j, 1), :], (8, 128))
+        tile_up = tile_of - below
+        zero = jnp.zeros((8, 128), F32)
+        place, found = zero, [zero] * 4
         for tile in range(TILES):
             cols = slice(128 * tile, 128 * tile + 128)
-            sources = (cst[:, cols], innov[0:8, cols], innov[8:16, cols], obsw[0:8, cols], obsw[8:16, cols])
             here = tile_of == tile + 1
             found = [
-                jnp.where(here, jnp.take_along_axis(source, lane, axis=1, mode="promise_in_bounds"), old)
-                for source, old in zip(sources, found)
+                jnp.where(here, lane_gather(source, lane), old)
+                for source, old in zip((innov[0:8, cols], innov[8:16, cols], obsw[0:8, cols], obsw[8:16, cols]), found)
             ]
-        first_i, second_i = split_pair(found[1], found[2], left)
-        first_o, second_o = split_pair(found[3], found[4], left)
-        rec[2 * j] = jnp.concatenate([found[0], first_i, first_o], axis=0)
-        rec[2 * j + 1] = jnp.concatenate([pltpu.roll(found[0], 64, axis=1), second_i, second_o], axis=0)
+            if tile % 2 == 0:
+                both = lane_gather(cst[:, 64 * tile : 64 * tile + 128], lane)
+                place = jnp.where(tile_up == tile + 1, both, place)
+        found_ref[j] = jnp.concatenate(found + [place], axis=0)
         return carry
 
     blocks(0, NDEV // 2, PACK_PAIRS, pair, 0)
+
+    def part(j, carry):
+        both = found_ref[j]
+        place = both[32:36] + both[36:40]
+        turned = pltpu.roll(place, 64, axis=1)
+        first_i, second_i = split_pair(both[0:8], both[8:16], left)
+        first_o, second_o = split_pair(both[16:24], both[24:32], left)
+        for q, parts in enumerate((
+            [first_i, first_o, jnp.where(left_row, place[0:1], turned[1:2]), place[2:3]],
+            [second_i, second_o, jnp.where(left_row, turned[0:1], place[1:2]), turned[2:3]],
+        )):
+            for row, value in zip((0, 8, 16, 17), parts):
+                rec[2 * j + q, row : row + value.shape[0], :] = value
+        return carry
+
+    blocks(0, NDEV // 2, 8, part, 0)
 
 
 def pack(owner, cell, weights, innov, obsw):
@@ -110,30 +150,44 @@
         ),
         in_specs=[pl.BlockSpec(memory_space=pltpu.VMEM)] * 5,
         out_specs=(pl.BlockSpec(memory_space=pltpu.VMEM),) * 2,
-        scratch_shapes=[pltpu.VMEM((NDEV, 128), jnp.int32), pltpu.VMEM((8, PROF), F32)],
+        scratch_shapes=[
+            pltpu.VMEM((NDEV, 128), jnp.int32),
+            pltpu.VMEM((NDEV // 2, 128), jnp.int32),
+            pltpu.VMEM((NDEV // 2, 128), jnp.int32),
+            pltpu.VMEM((8, PROF // 2), F32),
+            pltpu.VMEM((NDEV // 2, 40, 128), F32),
+        ],
         compiler_params=pltpu.CompilerParams(vmem_limit_bytes=VMEM_LIMIT),
         name="pack",
     )(owner, cell, weights, innov, obsw)
 
 
-def unpack_kernel(ret, owner, rank, innov, dep):
-    def one(o, found):
-        tile = ret[o]
-        new = []
-        for t in range(TILES):
-            idx = jnp.broadcast_to(rank[t : t + 1, :], (8, 128))
-            here = jnp.broadcast_to(owner[t : t + 1, :], (8, 128)) == o
-            low = jnp.take_along_axis(tile, idx, axis=1, mode="promise_in_bounds")
-            high = jnp.take_along_axis(tile, idx + 64, axis=1, mode="promise_in_bounds")
-            new.append(jnp.where(here, low, found[2 * t]))
-            new.append(jnp.where(here, high, found[2 * t + 1]))
-        return tuple(new)
-
-    found = blocks(0, NDEV, UNPACK_OWNERS, one, tuple(jnp.zeros((8, 128), F32) for _ in range(2 * TILES)))
-    for t in range(TILES):
-        cols = slice(128 * t, 128 * t + 128)
-        dep[0:8, cols] = found[2 * t] - innov[0:8, cols]
-        dep[8:16, cols] = found[2 * t + 1] - innov[8:16, cols]
+def unpack_kernel(ret, owner, rank, innov, dep, low_ref, high_ref):
+    left = lane_iota(8) < 64
+
+    def pair(j, carry):
+        one, two = ret[2 * j], ret[2 * j + 1]
+        low_ref[j] = jnp.where(left, one, pltpu.roll(two, 64, axis=1))
+        high_ref[j] = jnp.where(left, pltpu.roll(one, 64, axis=1), two)
+        return carry
+
+    blocks(0, NDEV // 2, 16, pair, 0)
+
+    def tile(t, carry):
+        owners = jnp.broadcast_to(owner[pl.ds(t, 1), :], (8, 128))
+        lane = jnp.broadcast_to(rank[pl.ds(t, 1), :], (8, 128)) + 64 * (owners % 2)
+        pair_of = owners // 2
+        low = high = jnp.zeros((8, 128), F32)
+        for j in range(NDEV // 2):
+            here = pair_of == j
+            low = jnp.where(here, lane_gather(low_ref[j], lane), low)
+            high = jnp.where(here, lane_gather(high_ref[j], lane), high)
+        cols = pl.ds(pl.multiple_of(128 * t, 128), 128)
+        dep[0:8, cols] = low - innov[0:8, cols]
+        dep[8:16, cols] = high - innov[8:16, cols]
+        return carry
+
+    blocks(0, TILES, UNPACK_TILES, tile, 0)
 
 
 def unpack(ret, owner, rank, innov):
@@ -142,6 +196,7 @@
         out_shape=jax.ShapeDtypeStruct((LEV, PROF), F32),
         in_specs=[pl.BlockSpec(memory_space=pltpu.VMEM)] * 4,
         out_specs=pl.BlockSpec(memory_space=pltpu.VMEM),
+        scratch_shapes=[pltpu.VMEM((NDEV // 2, 8, 128), F32)] * 2,
         compiler_params=pltpu.CompilerParams(vmem_limit_bytes=VMEM_LIMIT),
         name="unpack",
     )(ret, owner, rank, innov)
@@ -223,18 +278,6 @@
 def prev_cols(parts, first):
     rolled = [pltpu.roll(part, 1, axis=1) for part in parts]
     return [jnp.where(first, rolled[(i + 2) % 3], rolled[i]) for i in range(3)]
-
-
-def blocks(start, count, width, body, carry):
-    def many(i, carry):
-        for q in range(width):
-            carry = body(start + width * i + q, carry)
-        return carry
-
-    carry = lax.fori_loop(0, count // width, many, carry)
-    for q in range(count - count % width, count):
-        carry = body(start + q, carry)
-    return carry
 
 
 def build_faces(coef, coef_side, gy):
@@ -381,21 +424,28 @@
 
 def observe_all(recv, field3, adj, ret_send):
     left = lane_iota(8) < 64
-    rows_b = lax.broadcasted_iota(jnp.int32, (CY, 256), 0).astype(F32)
-    rows_a = lax.broadcasted_iota(jnp.int32, (CX, 256), 0).astype(F32)
+    left_row = lane_iota(1) < 64
+    width = OBSERVE_TILES * 128
+    rows_b = lax.broadcasted_iota(jnp.int32, (CY, width), 0).astype(F32)
+    rows_a = lax.broadcasted_iota(jnp.int32, (CX, width), 0).astype(F32)
 
     def observe(i, carry):
-        pairs = []
-        for h in range(2):
-            one, two = recv[4 * i + 2 * h], recv[4 * i + 2 * h + 1]
-            place = jnp.where(left, one[0:8], pltpu.roll(two[0:8], 64, axis=1))
-            low_i = jnp.where(left, one[8:16], pltpu.roll(two[8:16], 64, axis=1))
-            high_i = jnp.where(left, pltpu.roll(one[8:16], 64, axis=1), two[8:16])
-            low_o = jnp.where(left, one[16:24], pltpu.roll(two[16:24], 64, axis=1))
-            high_o = jnp.where(left, pltpu.roll(one[16:24], 64, axis=1), two[16:24])
-            pairs.append((place, jnp.concatenate([low_i, high_i], axis=0), jnp.concatenate([low_o, high_o], axis=0)))
-        place, innov, obsw = [jnp.concatenate([pairs[0][n], pairs[1][n]], axis=1) for n in range(3)]
-        cell, along_x, along_y = place[0:1], place[1:2], place[2:3]
+        parts = []
+        for h in range(OBSERVE_TILES):
+            one, two = recv[2 * (OBSERVE_TILES * i + h)], recv[2 * (OBSERVE_TILES * i + h) + 1]
+            turned_one, turned_two = pltpu.roll(one, 64, axis=1), pltpu.roll(two, 64, axis=1)
+            parts.append((
+                jnp.where(left_row, one[16:17], turned_two[16:17]),
+                jnp.where(left_row, turned_one[16:17], two[16:17]),
+                jnp.where(left_row, one[17:18], turned_two[17:18]),
+                jnp.where(left, one[0:8], turned_two[0:8]),
+                jnp.where(left, turned_one[0:8], two[0:8]),
+                jnp.where(left, one[8:16], turned_two[8:16]),
+                jnp.where(left, turned_one[8:16], two[8:16]),
+            ))
+        cell, along_x, along_y, low_i, high_i, low_o, high_o = [jnp.concatenate(part, axis=1) for part in zip(*parts)]
+        innov = jnp.concatenate([low_i, high_i], axis=0)
+        obsw = jnp.concatenate([low_o, high_o], axis=0)
         cell_a = jnp.floor(cell * (1.0 / CY))
         cell_b = cell - CY * cell_a
         from_a = rows_a - cell_a
@@ -404,17 +454,19 @@
         in_y = jnp.where(from_b == 0.0, 1.0 - along_y, jnp.where(from_b == 1.0, along_y, 0.0))
         y_high = in_y.astype(BF16)
         y_low = (in_y - y_high.astype(F32)).astype(BF16)
-        rows = jnp.dot(
-            field3[...], jnp.concatenate([y_high, y_low, y_high], axis=0), preferred_element_type=F32
-        )
-        vals = jnp.sum(rows.reshape(LEV, CX, 256) * in_x[None], axis=1)
+        y_rows = jnp.concatenate([y_high, y_low, y_high], axis=0)
+        vals = []
+        for k in range(0, LEV, 4):
+            rows = jnp.dot(field3[CX * k : CX * (k + 4), :], y_rows, preferred_element_type=F32)
+            vals.append(jnp.sum(rows.reshape(4, CX, width) * in_x[None], axis=1))
+        vals = jnp.concatenate(vals, axis=0)
         forcing = obsw * (vals - innov)
-        for h in range(2):
+        for h in range(OBSERVE_TILES):
             cols = slice(128 * h, 128 * h + 128)
             first, second = split_pair(vals[0:8, cols], vals[8:16, cols], left)
-            ret_send[4 * i + 2 * h] = first
-            ret_send[4 * i + 2 * h + 1] = second
-        spread = (in_x[None] * forcing[:, None, :]).reshape(LEV * CX, 256)
+            ret_send[2 * (OBSERVE_TILES * i + h)] = first
+            ret_send[2 * (OBSERVE_TILES * i + h) + 1] = second
+        spread = (in_x[None] * forcing[:, None, :]).reshape(LEV * CX, width)
         high = spread.astype(BF16)
         low = (spread - high.astype(F32)).astype(BF16)
         adj[...] += lax.dot_general(
@@ -425,7 +477,7 @@
         )
         return carry
 
-    lax.fori_loop(0, NDEV // 4, observe, 0)
+    lax.fori_loop(0, NDEV // 2 // OBSERVE_TILES, observe, 0)
 
 
 def main_kernel(

time: 177 us -> 124 us (0.70)
  Pallas kernels: 173 us -> 119 us
    pallas_call x1, Pallas kernels: 140 us -> 104 us  [gradient_call(): pl.pallas_call(main_kernel, out_shape=(jax.ShapeDtypeStruct((LEV, CX, CY)...]
    pallas_call x1, Pallas kernels: 14.4 us -> 5.07 us  [unpack(): pl.pallas_call(unpack_kernel, out_shape=jax.ShapeDtypeStruct((LEV, PROF),...]
    pallas_call x1, Pallas kernels: 17.7 us -> 9.82 us  [pack(): pl.pallas_call(pack_kernel, out_shape=(jax.ShapeDtypeStruct((NDEV, REC, 1...]
where the time goes in v2:
time: 124 us; the launch traced here: 123 us
  Pallas kernels  119 us (96%)
  local copies, waits for them, and re-layouts  3.27 us (3%)
    pallas_call x1, Pallas kernels, gradient_call(): pl.pallas_call(main_kernel, out_shape=(jax.ShapeDtypeStruct((LEV, CX, CY)...  104 us
    pallas_call x1, Pallas kernels, pack(): pl.pallas_call(pack_kernel, out_shape=(jax.ShapeDtypeStruct((NDEV, REC, 1...  9.82 us
    pallas_call x1, Pallas kernels, unpack(): pl.pallas_call(unpack_kernel, out_shape=jax.ShapeDtypeStruct((LEV, PROF),...  5.07 us
    unnamed x4, local copies, waits for them, and re-layouts  3.27 us

profile of v2, /device:TPU:1, one launch (start us, length us, event | category | flops | bytes accessed | tf_op | source)
XLA Modules:
  0.0 123.3 jit_solution(10368061345010415071)
XLA Ops:
  0.6 9.8 %pack.1 = (f32[128,18,128]{2,1,0:T(8,128)}, s32[16,128]{1,0:T(8,128)}) custom-call(s32[16,128]{1,0:T(8,128)} %bitcast.2, s32[16,128]{1,0:T(8,128)} %bitcast.4, f32[4,2048]{1,0:T(4,128)} %weights.1, f32[16,2048]{1,0:T(8,128)} %innov.3, f32[16,2048]{1,0:T(8,128)} %obsw.1), custom_call_target="tpu_custom_call" | custom-call | tf_op jit(solution)/shard_map/pack/pallas_call | solution.py:145
  10.5 104.5 %gradient.1 = (f32[16,64,256]{2,1,0:T(8,128)}, f32[128,8,128]{2,1,0:T(8,128)}, f32[16,64,256]{2,1,0:T(8,128)}) custom-call(f32[16,64,256]{2,1,0:T(8,128)} %control.1, f32[16,64,256]{2,1,0:T(8,128)} %sigma.1, f32[15,64,256]{2,1,0:T(8,128)} %vert.1, f32[64,256]{1,0:T(8,128)} %zonal.1, f32[64,256]{1,0:T(8,128)} %merid.1, s32[64,256]{1,0:T(8,128)} %mask.1, ...), custom_call_target="tpu_custom_call" | custom-call | tf_op jit(solution)/shard_map/gradient/pallas_call | solution.py:627
  114.9 0.0 copy-start
  114.9 5.1 %unpack.1 = f32[16,2048]{1,0:T(8,128)} custom-call(f32[128,8,128]{2,1,0:T(8,128)} %get-tuple-element.10.ret, s32[16,128]{1,0:T(8,128)} %bitcast.3, s32[16,128]{1,0:T(8,128)} %get-tuple-element.11.rank, f32[16,2048]{1,0:T(8,128)} %innov.3), custom_call_target="tpu_custom_call" | custom-call | tf_op jit(solution)/shard_map/unpack/pallas_call | solution.py:194
  120.0 2.3 %copy.16 = f32[16,64,256]{2,1,0:T(8,128)} copy(f32[16,64,256]{2,1,0:T(8,128)} %get-tuple-element.16) | data formatting | bytes 2097152
  122.3 0.0 copy-done
  122.3 1.0 copy.17
Async XLA Ops:
  114.9 7.4 %copy-start = (f32[16,64,256]{2,1,0:T(8,128)S(1)}, f32[16,64,256]{2,1,0:T(8,128)}, u32[]{:S(2)}) copy-start(f32[16,64,256]{2,1,0:T(8,128)} %get-tuple-element.18) | copy-start | bytes 3145732

commit v3 on v2

--- a/solution.py
+++ b/solution.py
@@ -59,7 +59,7 @@
     return first, second
 
 
-def pack_kernel(owner, cell, weights, innov, obsw, rec, rank_out, tab, lanes, tiles, cst, found_ref):
+def slot_table(owner, cell, weights, rank_out, tab, lanes, tiles, cst):
     rows_o = lax.broadcasted_iota(jnp.int32, (NDEV, 256), 0)
     before = (
         lax.broadcasted_iota(jnp.int32, (256, 256), 0) < lax.broadcasted_iota(jnp.int32, (256, 256), 1)
@@ -99,11 +99,14 @@
         cst[row + 1 : row + 2, to] = weights[1:2, cols] + weights[3:4, cols]
         cst[row + 2 : row + 3, to] = weights[2:3, cols] + weights[3:4, cols]
 
+
+def pack_records(j0, innov, obsw, lanes, tiles, cst, found_ref, rec):
     left = lane_iota(8) < 64
     left_row = lane_iota(1) < 64
     below = lax.broadcasted_iota(jnp.int32, (8, 128), 0) // 4
 
-    def pair(j, carry):
+    for q in range(PACK_PAIRS):
+        j = (j0 + q) % (NDEV // 2)
         lane = jnp.broadcast_to(lanes[pl.ds(j, 1), :], (8, 128))
         tile_of = jnp.broadcast_to(tiles[pl.ds(j, 1), :], (8, 128))
         tile_up = tile_of - below
@@ -119,50 +122,24 @@
             if tile % 2 == 0:
                 both = lane_gather(cst[:, 64 * tile : 64 * tile + 128], lane)
                 place = jnp.where(tile_up == tile + 1, both, place)
-        found_ref[j] = jnp.concatenate(found + [place], axis=0)
-        return carry
-
-    blocks(0, NDEV // 2, PACK_PAIRS, pair, 0)
-
-    def part(j, carry):
-        both = found_ref[j]
+        found_ref[q] = jnp.concatenate(found + [place], axis=0)
+
+    for q in range(PACK_PAIRS):
+        j = (j0 + q) % (NDEV // 2)
+        both = found_ref[q]
         place = both[32:36] + both[36:40]
         turned = pltpu.roll(place, 64, axis=1)
         first_i, second_i = split_pair(both[0:8], both[8:16], left)
         first_o, second_o = split_pair(both[16:24], both[24:32], left)
-        for q, parts in enumerate((
+        for side, parts in enumerate((
             [first_i, first_o, jnp.where(left_row, place[0:1], turned[1:2]), place[2:3]],
             [second_i, second_o, jnp.where(left_row, turned[0:1], place[1:2]), turned[2:3]],
         )):
             for row, value in zip((0, 8, 16, 17), parts):
-                rec[2 * j + q, row : row + value.shape[0], :] = value
-        return carry
-
-    blocks(0, NDEV // 2, 8, part, 0)
-
-
-def pack(owner, cell, weights, innov, obsw):
-    return pl.pallas_call(
-        pack_kernel,
-        out_shape=(
-            jax.ShapeDtypeStruct((NDEV, REC, 128), F32),
-            jax.ShapeDtypeStruct((TILES, 128), jnp.int32),
-        ),
-        in_specs=[pl.BlockSpec(memory_space=pltpu.VMEM)] * 5,
-        out_specs=(pl.BlockSpec(memory_space=pltpu.VMEM),) * 2,
-        scratch_shapes=[
-            pltpu.VMEM((NDEV, 128), jnp.int32),
-            pltpu.VMEM((NDEV // 2, 128), jnp.int32),
-            pltpu.VMEM((NDEV // 2, 128), jnp.int32),
-            pltpu.VMEM((8, PROF // 2), F32),
-            pltpu.VMEM((NDEV // 2, 40, 128), F32),
-        ],
-        compiler_params=pltpu.CompilerParams(vmem_limit_bytes=VMEM_LIMIT),
-        name="pack",
-    )(owner, cell, weights, innov, obsw)
-
-
-def unpack_kernel(ret, owner, rank, innov, dep, low_ref, high_ref):
+                rec[2 * j + side, row : row + value.shape[0], :] = value
+
+
+def unpack(ret, owner, rank, innov, dep, low_ref, high_ref):
     left = lane_iota(8) < 64
 
     def pair(j, carry):
@@ -188,18 +165,6 @@
         return carry
 
     blocks(0, TILES, UNPACK_TILES, tile, 0)
-
-
-def unpack(ret, owner, rank, innov):
-    return pl.pallas_call(
-        unpack_kernel,
-        out_shape=jax.ShapeDtypeStruct((LEV, PROF), F32),
-        in_specs=[pl.BlockSpec(memory_space=pltpu.VMEM)] * 4,
-        out_specs=pl.BlockSpec(memory_space=pltpu.VMEM),
-        scratch_shapes=[pltpu.VMEM((NDEV // 2, 8, 128), F32)] * 2,
-        compiler_params=pltpu.CompilerParams(vmem_limit_bytes=VMEM_LIMIT),
-        name="unpack",
-    )(ret, owner, rank, innov)
 
 
 def pack_sides(main, low_side, high_side, lev):
@@ -422,14 +387,17 @@
             grad[k, rows, :] = control[k, rows, :] + wet * value
 
 
-def observe_all(recv, field3, adj, ret_send):
+def observe_all(me, recv, field3, adj, ret_send, send):
     left = lane_iota(8) < 64
     left_row = lane_iota(1) < 64
     width = OBSERVE_TILES * 128
     rows_b = lax.broadcasted_iota(jnp.int32, (CY, width), 0).astype(F32)
     rows_a = lax.broadcasted_iota(jnp.int32, (CX, width), 0).astype(F32)
 
-    def observe(i, carry):
+    groups = NDEV // 2 // OBSERVE_TILES
+
+    def observe(n, carry):
+        i = (n + me // (2 * OBSERVE_TILES)) % groups
         parts = []
         for h in range(OBSERVE_TILES):
             one, two = recv[2 * (OBSERVE_TILES * i + h)], recv[2 * (OBSERVE_TILES * i + h) + 1]
@@ -466,6 +434,7 @@
             first, second = split_pair(vals[0:8, cols], vals[8:16, cols], left)
             ret_send[2 * (OBSERVE_TILES * i + h)] = first
             ret_send[2 * (OBSERVE_TILES * i + h) + 1] = second
+        lax.fori_loop(2 * OBSERVE_TILES * i, 2 * OBSERVE_TILES * (i + 1), send, 0)
         spread = (in_x[None] * forcing[:, None, :]).reshape(LEV * CX, width)
         high = spread.astype(BF16)
         low = (spread - high.astype(F32)).astype(BF16)
@@ -477,12 +446,13 @@
         )
         return carry
 
-    lax.fori_loop(0, NDEV // 2 // OBSERVE_TILES, observe, 0)
+    lax.fori_loop(0, groups, observe, 0)
 
 
 def main_kernel(
-    control, sigma, vert, zonal, merid, mask, rec, inc, ret, grad,
-    recv, ret_send, coef, coef_side, coef_low, coef_high, coef_from_high, coef_from_low,
+    control, sigma, vert, zonal, merid, mask, owner, cell, weights, innov, obsw, inc, dep, grad,
+    rec, recv, ret_send, ret, rank, tab, lanes, tiles, cst, found_ref, ret_low, ret_high,
+    coef, coef_side, coef_low, coef_high, coef_from_high, coef_from_low,
     main_a, side_a, main_b, side_b, main_c, side_c,
     low_a, high_a, from_high_a, from_low_a, low_c, high_c, from_high_c, from_low_c,
     upper, inverse, reduced, field3, adj,
@@ -499,19 +469,32 @@
         return carry
 
     lax.fori_loop(1, NDEV, greet, 0)
-    pl.semaphore_wait(barrier, NDEV - 1)
-
-    def rec_copy(to):
+
+    def to_device(src, dst, send_sem, recv_sem, to):
         return pltpu.make_async_remote_copy(
-            src_ref=rec.at[to], dst_ref=recv.at[me], send_sem=rec_send_sem, recv_sem=rec_recv_sem,
+            src_ref=src, dst_ref=dst, send_sem=send_sem, recv_sem=recv_sem,
             device_id=(to // NGY, to % NGY), device_id_type=MESH,
         )
 
-    def ret_copy(to):
-        return pltpu.make_async_remote_copy(
-            src_ref=ret_send.at[to], dst_ref=ret.at[me], send_sem=ret_send_sem, recv_sem=ret_recv_sem,
-            device_id=(to // NGY, to % NGY), device_id_type=MESH,
-        )
+    def send_rec(to, carry):
+        @pl.when(to != me)
+        def _():
+            to_device(rec.at[to], recv.at[me], rec_send_sem, rec_recv_sem, to).start()
+
+        return carry
+
+    def send_ret(to, carry):
+        @pl.when(to != me)
+        def _():
+            to_device(ret_send.at[to], ret.at[me], ret_send_sem, ret_recv_sem, to).start()
+
+        return carry
+
+    def wait_all(src, dst, send_sem, recv_sem):
+        most = pl.ds(0, NDEV - 1)
+        whole = to_device(src.at[most], dst.at[most], send_sem, recv_sem, me)
+        whole.wait_recv()
+        whole.wait_send()
 
     for half in range(2):
         coef[half, STEPS * 8 : (STEPS + CX) * 8, :] = jnp.zeros((CX * 8, 128), F32)
@@ -521,25 +504,31 @@
         store_level(coef, 1, x, 8, SOLVE_ROWS, merid[rows, :])
         store_level(coef, 2, x, 8, SOLVE_ROWS, mask[rows, :].astype(F32))
     pack_sides(coef, coef_low, coef_high, 8)
+    solve_first(control, vert, mask, upper, inverse, reduced, main_a)
+    pack_sides(main_a, low_a, high_a, LEV)
+
+    pl.semaphore_wait(barrier, NDEV - 1)
     coef_copies = halo_copies(
         coef, coef_low, coef_high, coef_from_high, coef_from_low, halo_send.at[0], halo_recv.at[0], gx, gy, 8
     )
-    for copy in coef_copies:
-        copy.start()
-
-    solve_first(control, vert, mask, upper, inverse, reduced, main_a)
-    pack_sides(main_a, low_a, high_a, LEV)
     field_copies = halo_copies(
         main_a, low_a, high_a, from_high_a, from_low_a, halo_send.at[1], halo_recv.at[1], gx, gy, LEV
     )
-    for copy in field_copies:
+    for copy in coef_copies + field_copies:
         copy.start()
 
-    def send_rec(d, carry):
-        rec_copy((me + d) % NDEV).start()
-        return carry
-
-    lax.fori_loop(1, NDEV, send_rec, 0)
+    slot_table(owner, cell, weights, rank, tab, lanes, tiles, cst)
+
+    def pack_some(n, carry):
+        j0 = (me // 2 + n * PACK_PAIRS) % (NDEV // 2)
+        pack_records(j0, innov, obsw, lanes, tiles, cst, found_ref, rec)
+
+        def send_one(q, carry):
+            return send_rec((2 * j0 + q) % NDEV, carry)
+
+        return lax.fori_loop(0, 2 * PACK_PAIRS, send_one, carry)
+
+    lax.fori_loop(0, NDEV // 2 // PACK_PAIRS, pack_some, 0)
     own = pltpu.make_async_copy(rec.at[me], recv.at[me], self_sem)
     own.start()
 
@@ -565,17 +554,13 @@
         return carry
 
     lax.fori_loop(0, LEV, scale, 0)
+    adj[...] = jnp.zeros_like(adj)
 
     own.wait()
-    whole = pltpu.make_async_remote_copy(
-        src_ref=rec.at[pl.ds(0, NDEV - 1)], dst_ref=recv.at[pl.ds(0, NDEV - 1)],
-        send_sem=rec_send_sem, recv_sem=rec_recv_sem, device_id=(gx, gy), device_id_type=MESH,
-    )
-    whole.wait_recv()
-    whole.wait_send()
-
-    adj[...] = jnp.zeros_like(adj)
-    observe_all(recv, field3, adj, ret_send)
+    wait_all(rec, recv, rec_send_sem, rec_recv_sem)
+    observe_all(me, recv, field3, adj, ret_send, send_ret)
+    own = pltpu.make_async_copy(ret_send.at[me], ret.at[me], self_sem)
+    own.start()
 
     def weigh(k, carry):
         for x in range(0, CX, SOLVE_ROWS):
@@ -591,13 +576,9 @@
     for copy in adj_copies:
         copy.start()
 
-    def send_ret(d, carry):
-        ret_copy((me + d) % NDEV).start()
-        return carry
-
-    lax.fori_loop(1, NDEV, send_ret, 0)
-    own = pltpu.make_async_copy(ret_send.at[me], ret.at[me], self_sem)
-    own.start()
+    own.wait()
+    wait_all(ret_send, ret, ret_send_sem, ret_recv_sem)
+    unpack(ret, owner, rank, innov, dep, ret_low, ret_high)
 
     for copy in adj_copies:
         copy.wait()
@@ -605,16 +586,8 @@
     diffuse(main_c, side_c, main_b, side_b, coef, coef_side)
     solve_last(main_c, control, vert, mask, upper, inverse, reduced, grad)
 
-    own.wait()
-    whole = pltpu.make_async_remote_copy(
-        src_ref=ret_send.at[pl.ds(0, NDEV - 1)], dst_ref=ret.at[pl.ds(0, NDEV - 1)],
-        send_sem=ret_send_sem, recv_sem=ret_recv_sem, device_id=(gx, gy), device_id_type=MESH,
-    )
-    whole.wait_recv()
-    whole.wait_send()
-
-
-def gradient_call(control, sigma, vert, zonal, merid, mask, rec):
+
+def gradient_call(*args):
     vmem = pl.BlockSpec(memory_space=pltpu.VMEM)
 
     def field(rows, lanes, lev=LEV):
@@ -628,14 +601,24 @@
         main_kernel,
         out_shape=(
             jax.ShapeDtypeStruct((LEV, CX, CY), F32),
-            jax.ShapeDtypeStruct((NDEV, 8, 128), F32),
+            jax.ShapeDtypeStruct((LEV, PROF), F32),
             jax.ShapeDtypeStruct((LEV, CX, CY), F32),
         ),
-        in_specs=[vmem] * 7,
+        in_specs=[vmem] * 11,
         out_specs=(vmem,) * 3,
         scratch_shapes=[
             pltpu.VMEM((NDEV, REC, 128), F32),
+            pltpu.VMEM((NDEV, REC, 128), F32),
             pltpu.VMEM((NDEV, 8, 128), F32),
+            pltpu.VMEM((NDEV, 8, 128), F32),
+            pltpu.VMEM((TILES, 128), jnp.int32),
+            pltpu.VMEM((NDEV, 128), jnp.int32),
+            pltpu.VMEM((NDEV // 2, 128), jnp.int32),
+            pltpu.VMEM((NDEV // 2, 128), jnp.int32),
+            pltpu.VMEM((8, PROF // 2), F32),
+            pltpu.VMEM((PACK_PAIRS, 40, 128), F32),
+            pltpu.VMEM((NDEV // 2, 8, 128), F32),
+            pltpu.VMEM((NDEV // 2, 8, 128), F32),
             field(ROWS, 256, 8), field(SROWS, 128, 8), *sides(8),
             field(ROWS, 256), field(SROWS, 128),
             field(ROWS, 256), field(SROWS, 128),
@@ -654,18 +637,14 @@
             collective_id=0, has_side_effects=True, vmem_limit_bytes=VMEM_LIMIT
         ),
         name="gradient",
-    )(control, sigma, vert, zonal, merid, mask, rec)
+    )(*args)
 
 
 def shards(control, sigma, vert_diff, zonal_diff, merid_diff, ocean_mask, owner, cell, interp_weights, innovation, obs_weight):
-    owner_rows = owner.reshape(TILES, 128)
-    cell_rows = cell.reshape(TILES, 128)
-    rec, rank = pack(owner_rows, cell_rows, interp_weights, innovation, obs_weight)
-    increment, ret, gradient = gradient_call(
-        control, sigma, vert_diff, zonal_diff, merid_diff, ocean_mask, rec
+    return gradient_call(
+        control, sigma, vert_diff, zonal_diff, merid_diff, ocean_mask,
+        owner.reshape(TILES, 128), cell.reshape(TILES, 128), interp_weights, innovation, obs_weight,
     )
-    departures = unpack(ret, owner_rows, rank, innovation)
-    return increment, departures, gradient
 
 
 def solution(mesh):

time: 124 us -> 111 us (0.90)
  Pallas kernels: 119 us -> 105 us
    pallas_call x2 -> x0, Pallas kernels: 14.9 us -> none  [the longest x1 9.82 us: pack(): pl.pallas_call(pack_kernel, out_shape=(jax.ShapeDtypeStruct((NDEV, REC, 1...]
    unnamed x4 -> x7, local copies, waits for them, and re-layouts: 3.27 us -> 4.02 us
where the time goes in v3:
time: 111 us; the launch traced here: 110 us
  Pallas kernels  105 us (95%)
  local copies, waits for them, and re-layouts  4.02 us (4%)
    pallas_call x1, Pallas kernels, gradient_call(): pl.pallas_call(main_kernel, out_shape=(jax.ShapeDtypeStruct((LEV, CX, CY)...  105 us
    unnamed x7, local copies, waits for them, and re-layouts  4.02 us

profile of v3, /device:TPU:1, one launch (start us, length us, event | category | flops | bytes accessed | tf_op | source)
XLA Modules:
  0.0 109.9 jit_solution(10215018498890473102)
XLA Ops:
  0.6 105.2 %gradient.1 = (f32[16,64,256]{2,1,0:T(8,128)}, f32[16,2048]{1,0:T(8,128)}, f32[16,64,256]{2,1,0:T(8,128)}) custom-call(f32[16,64,256]{2,1,0:T(8,128)} %control.1, f32[16,64,256]{2,1,0:T(8,128)} %sigma.1, f32[15,64,256]{2,1,0:T(8,128)} %vert.1, f32[64,256]{1,0:T(8,128)} %zonal.1, f32[64,256]{1,0:T(8,128)} %merid.1, s32[64,256]{1,0:T(8,128)} %mask.1, ...), custom_call_target="tpu_custom_call" | custom-call | tf_op jit(solution)/shard_map/gradient/pallas_call | solution.py:600
  105.8 0.0 copy-start.1
  105.8 0.0 copy-start
  105.8 2.4 %copy.17 = f32[16,64,256]{2,1,0:T(8,128)} copy(f32[16,64,256]{2,1,0:T(8,128)} %get-tuple-element.6) | data formatting | bytes 2097152
  108.2 0.0 copy-done.1
  108.2 0.7 copy.18
  108.9 0.0 copy-done
  108.9 1.0 copy.19
Async XLA Ops:
  105.8 2.4 %copy-start.1 = (f32[16,2048]{1,0:T(8,128)S(1)}, f32[16,2048]{1,0:T(8,128)}, u32[]{:S(2)}) copy-start(f32[16,2048]{1,0:T(8,128)} %get-tuple-element.7) | copy-start | bytes 393220
  105.8 3.1 %copy-start = (f32[16,64,256]{2,1,0:T(8,128)S(1)}, f32[16,64,256]{2,1,0:T(8,128)}, u32[]{:S(2)}) copy-start(f32[16,64,256]{2,1,0:T(8,128)} %get-tuple-element.8) | copy-start | bytes 3145732

commit v4 on v3

--- a/solution.py
+++ b/solution.py
@@ -27,7 +27,12 @@
 SROWS = 96
 GROUPS = 12
 REC = 18
-DIFFUSE_ROWS = 16
+DIFFUSE_TILES = 4
+SEG = 11
+ALL_ROWS = 8 * SEG
+EDGE = 24
+COLS = CY + 2 * EDGE
+PAIR_STRIDE = 21
 PACK_PAIRS = 8
 OBSERVE_TILES = 8
 UNPACK_TILES = 2
@@ -106,7 +111,7 @@
     below = lax.broadcasted_iota(jnp.int32, (8, 128), 0) // 4
 
     for q in range(PACK_PAIRS):
-        j = (j0 + q) % (NDEV // 2)
+        j = lax.rem(j0 + q * PAIR_STRIDE, NDEV // 2)
         lane = jnp.broadcast_to(lanes[pl.ds(j, 1), :], (8, 128))
         tile_of = jnp.broadcast_to(tiles[pl.ds(j, 1), :], (8, 128))
         tile_up = tile_of - below
@@ -125,7 +130,7 @@
         found_ref[q] = jnp.concatenate(found + [place], axis=0)
 
     for q in range(PACK_PAIRS):
-        j = (j0 + q) % (NDEV // 2)
+        j = lax.rem(j0 + q * PAIR_STRIDE, NDEV // 2)
         both = found_ref[q]
         place = both[32:36] + both[36:40]
         turned = pltpu.roll(place, 64, axis=1)
@@ -240,17 +245,12 @@
     return [jnp.where(last, rolled[(i + 1) % 3], rolled[i]) for i in range(3)]
 
 
-def prev_cols(parts, first):
-    rolled = [pltpu.roll(part, 1, axis=1) for part in parts]
-    return [jnp.where(first, rolled[(i + 2) % 3], rolled[i]) for i in range(3)]
-
-
 def build_faces(coef, coef_side, gy):
     lane = lane_iota(1)
     first_part = jnp.where(gy < NGY - 1, 1.0, 0.0).astype(F32)
     last_part = jnp.where(gy > 0, 1.0, 0.0).astype(F32)
     inside = jnp.where(lane < 64, first_part, last_part)
-    last, first = lane == 127, lane == 0
+    last = lane == 127
 
     def row(r, which):
         at = pl.ds(r * 8 + which, 1)
@@ -270,56 +270,90 @@
         ahead = wet_row(r + 1)
         zonal, merid = row(r, 0), row(r, 1)
         north = next_cols(wet, last)
-        south = prev_cols(wet, first)
-        merid_south = prev_cols(merid, first)
         put(r, 0, [z * w * a for z, w, a in zip(zonal, wet, ahead)])
         put(r, 1, [m * w * n for m, w, n in zip(merid, wet, north)])
-        put(r, 3, [m * w * n for m, w, n in zip(merid_south, south, wet)])
         return tuple(ahead)
 
     blocks(0, ROWS - 1, 8, one, tuple(wet_row(0)))
 
 
-def diffuse(first_main, first_side, second_main, second_side, coef, coef_side):
-    lane = lane_iota(LEV)
-    last, first = lane == 127, lane == 0
-
-    def face(r, which):
-        at = pl.ds(r * 8 + which, 1)
-        parts = [coef[0, at, :], coef[1, at, :], coef_side[pl.ds((r + SPAD) * 8 + which, 1), :]]
-        return [jnp.broadcast_to(part, (LEV, 128)) for part in parts]
+def put_columns(plane, parts):
+    first, second, side = [part.T for part in parts]
+    plane[EDGE : EDGE + 128, :] = first
+    plane[EDGE + 128 : EDGE + 256, :] = second
+    plane[EDGE + CY : EDGE + CY + 16, :] = side[0:16]
+    plane[EDGE - 16 : EDGE, :] = side[112:128]
+
+
+def expand_faces(coef, coef_side, face_x, face_y):
+    def one(place, carry):
+        for which, planes, to in ((0, face_x, place + 1), (1, face_y, place)):
+            parts = []
+            for ref, pad in ((coef.at[0], 0), (coef.at[1], 0), (coef_side, SPAD)):
+                rows = [ref[pl.ds((SEG * seg + place + pad) * 8 + which, 1), :] for seg in range(8)]
+                parts.append(jnp.concatenate([jnp.broadcast_to(row, (LEV, 128)) for row in rows], axis=0))
+            put_columns(planes.at[to], parts)
+        return carry
+
+    blocks(0, SEG, 2, one, 0)
+    face_x[0] = pltpu.roll(face_x[SEG], LEV, axis=1)
+
+
+def turn_edges(field):
+    field[0] = pltpu.roll(field[SEG], LEV, axis=1)
+    field[SEG + 1] = pltpu.roll(field[1], 128 - LEV, axis=1)
+
+
+def diffuse(main, side, field_a, field_b, face_x, face_y):
+    def enter(place, carry):
+        parts = []
+        for ref, pad in ((main.at[0], 0), (main.at[1], 0), (side, SPAD)):
+            rows = [pl.ds(pl.multiple_of((SEG * seg + place + pad) * LEV, LEV), LEV) for seg in range(8)]
+            parts.append(jnp.concatenate([ref[at, :] for at in rows], axis=0))
+        put_columns(field_a.at[place + 1], parts)
+        return carry
+
+    blocks(0, SEG, 4, enter, 0)
+    bottom = lax.broadcasted_iota(jnp.int32, (8, 128), 0) == 7
+    turn_edges(field_a)
 
     for step in range(STEPS):
-        even = step % 2 == 0
-        main, side = (first_main, first_side) if even else (second_main, second_side)
-        new_main, new_side = (second_main, second_side) if even else (first_main, first_side)
-        final = step == STEPS - 1
-
-        def field(r):
-            at = pl.ds(pl.multiple_of(r * LEV, LEV), LEV)
-            return [main[0, at, :], main[1, at, :], side[pl.ds(pl.multiple_of((r + SPAD) * LEV, LEV), LEV), :]]
-
-        def flux(r, here, ahead):
-            return [f * (a - h) for f, a, h in zip(face(r, 0), ahead, here)]
-
-        def one(r, carry):
-            here, behind = carry[:3], carry[3:]
-            ahead = field(r + 1)
-            east = flux(r, here, ahead)
-            north = [f * (n - h) for f, n, h in zip(face(r, 1), next_cols(here, last), here)]
-            south = [f * (h - p) for f, p, h in zip(face(r, 3), prev_cols(here, first), here)]
-            new = [h + ((e - w) + (n - s)) for h, e, w, n, s in zip(here, east, behind, north, south)]
-            at = pl.ds(pl.multiple_of(r * LEV, LEV), LEV)
-            new_main[0, at, :] = new[0]
-            new_main[1, at, :] = new[1]
-            if not final:
-                new_side[pl.ds(pl.multiple_of((r + SPAD) * LEV, LEV), LEV), :] = new[2]
-            return tuple(ahead) + tuple(east)
-
-        start = step + 1
-        here = field(start)
-        behind = flux(start - 1, field(start - 1), here)
-        blocks(start, ROWS - 2 * start, DIFFUSE_ROWS, one, tuple(here) + tuple(behind))
+        now, new = (field_a, field_b) if step % 2 == 0 else (field_b, field_a)
+
+        def north_flux(t, p, here):
+            row = pl.multiple_of(8 * t, 8)
+            return face_y[p - 1, pl.ds(row, 8), :] * (now[p, pl.ds(row + 1, 8), :] - here)
+
+        def tile(t, carry):
+            at = pl.ds(pl.multiple_of(8 * t, 8), 8)
+            here, west = now[1, at, :], face_x[0, at, :] * (now[1, at, :] - now[0, at, :])
+            norths = []
+            for p in range(1, SEG + 1):
+                ahead = now[p + 1, at, :]
+                east = face_x[p, at, :] * (ahead - here)
+                north = north_flux(t, p, here)
+                south = pltpu.roll(jnp.where(bottom, carry[p - 1], north), 1, axis=0)
+                new[p, at, :] = here + ((east - west) + (north - south))
+                here, west = ahead, east
+                norths.append(north)
+            return tuple(norths)
+
+        first = (EDGE - (STEPS - 1 - step)) // 8
+        last = (EDGE + CY + (STEPS - 1 - step) + 7) // 8
+        before = [north_flux(first - 1, p, now[p, 8 * first - 8 : 8 * first, :]) for p in range(1, SEG + 1)]
+        blocks(first, last - first, DIFFUSE_TILES, tile, tuple(before))
+        if step < STEPS - 1:
+            turn_edges(new)
+
+    def leave(place, carry):
+        for half in range(2):
+            rows = field_a[place + 1, EDGE + 128 * half : EDGE + 128 * half + 128, :].T
+            for seg in range(8):
+                at = pl.ds(pl.multiple_of((SEG * seg + place) * LEV, LEV), LEV)
+                main[half, at, :] = rows[LEV * seg : LEV * seg + LEV]
+        return carry
+
+    blocks(0, SEG, 4, leave, 0)
 
 
 SOLVE_ROWS = 32
@@ -387,7 +421,18 @@
             grad[k, rows, :] = control[k, rows, :] + wet * value
 
 
-def observe_all(me, recv, field3, adj, ret_send, send):
+def send_first(n, j, partner, send):
+    @pl.when(n > 0)
+    def _():
+        send(2 * j)
+        send(2 * j + 1)
+
+    @pl.when(n == 0)
+    def _():
+        send(partner)
+
+
+def observe_all(mine, partner, recv, field3, adj, ret_send, send):
     left = lane_iota(8) < 64
     left_row = lane_iota(1) < 64
     width = OBSERVE_TILES * 128
@@ -397,10 +442,10 @@
     groups = NDEV // 2 // OBSERVE_TILES
 
     def observe(n, carry):
-        i = (n + me // (2 * OBSERVE_TILES)) % groups
+        pairs = [lax.rem(mine + n + groups * h, NDEV // 2) for h in range(OBSERVE_TILES)]
         parts = []
         for h in range(OBSERVE_TILES):
-            one, two = recv[2 * (OBSERVE_TILES * i + h)], recv[2 * (OBSERVE_TILES * i + h) + 1]
+            one, two = recv[2 * pairs[h]], recv[2 * pairs[h] + 1]
             turned_one, turned_two = pltpu.roll(one, 64, axis=1), pltpu.roll(two, 64, axis=1)
             parts.append((
                 jnp.where(left_row, one[16:17], turned_two[16:17]),
@@ -432,9 +477,11 @@
         for h in range(OBSERVE_TILES):
             cols = slice(128 * h, 128 * h + 128)
             first, second = split_pair(vals[0:8, cols], vals[8:16, cols], left)
-            ret_send[2 * (OBSERVE_TILES * i + h)] = first
-            ret_send[2 * (OBSERVE_TILES * i + h) + 1] = second
-        lax.fori_loop(2 * OBSERVE_TILES * i, 2 * OBSERVE_TILES * (i + 1), send, 0)
+            ret_send[2 * pairs[h]] = first
+            ret_send[2 * pairs[h] + 1] = second
+        for h in range(1, OBSERVE_TILES):
+            send(2 * pairs[h])
+            send(2 * pairs[h] + 1)
         spread = (in_x[None] * forcing[:, None, :]).reshape(LEV * CX, width)
         high = spread.astype(BF16)
         low = (spread - high.astype(F32)).astype(BF16)
@@ -444,16 +491,19 @@
             (((1,), (1,)), ((), ())),
             preferred_element_type=F32,
         )
+        send_first(n, pairs[0], partner, send)
         return carry
 
     lax.fori_loop(0, groups, observe, 0)
 
 
 def main_kernel(
-    control, sigma, vert, zonal, merid, mask, owner, cell, weights, innov, obsw, inc, dep, grad,
+    control_in, sigma_in, vert_in, zonal_in, merid_in, mask_in, owner_in, cell_in, weights_in, innov_in, obsw_in,
+    inc_out, dep_out, grad_out,
+    control, sigma, vert, zonal, merid, mask, owner, cell, weights, innov, obsw, inc, dep, grad, io_sem,
     rec, recv, ret_send, ret, rank, tab, lanes, tiles, cst, found_ref, ret_low, ret_high,
     coef, coef_side, coef_low, coef_high, coef_from_high, coef_from_low,
-    main_a, side_a, main_b, side_b, main_c, side_c,
+    main_a, side_a, main_c, side_c, field_a, field_b, face_x, face_y,
     low_a, high_a, from_high_a, from_low_a, low_c, high_c, from_high_c, from_low_c,
     upper, inverse, reduced, field3, adj,
     rec_send_sem, rec_recv_sem, ret_send_sem, ret_recv_sem, self_sem, halo_send, halo_recv,
@@ -461,34 +511,42 @@
     gx, gy = lax.axis_index("gx"), lax.axis_index("gy")
     me = gx * NGY + gy
 
+    field_ins = ((zonal_in, zonal), (merid_in, merid), (mask_in, mask), (vert_in, vert), (control_in, control))
+    late_ins = ((owner_in, owner), (cell_in, cell), (weights_in, weights), (innov_in, innov), (obsw_in, obsw))
+    loads = [
+        pltpu.make_async_copy(src, dst, io_sem.at[n])
+        for n, (src, dst) in enumerate(field_ins + late_ins + ((sigma_in, sigma),))
+    ]
+    stores = [
+        pltpu.make_async_copy(src, dst, io_sem.at[len(loads) + n])
+        for n, (src, dst) in enumerate(((inc, inc_out), (dep, dep_out), (grad, grad_out)))
+    ]
+    for copy in loads:
+        copy.start()
+
     barrier = pltpu.get_barrier_semaphore()
 
     def greet(d, carry):
-        to = (me + d) % NDEV
-        pl.semaphore_signal(barrier, inc=1, device_id=(to // NGY, to % NGY), device_id_type=MESH)
-        return carry
-
-    lax.fori_loop(1, NDEV, greet, 0)
+        to = lax.rem(me + d, NDEV)
+        pl.semaphore_signal(barrier, inc=1, device_id=(lax.div(to, NGY), lax.rem(to, NGY)), device_id_type=MESH)
+        return carry
+
+    blocks(1, NDEV - 1, 8, greet, 0)
 
     def to_device(src, dst, send_sem, recv_sem, to):
         return pltpu.make_async_remote_copy(
             src_ref=src, dst_ref=dst, send_sem=send_sem, recv_sem=recv_sem,
-            device_id=(to // NGY, to % NGY), device_id_type=MESH,
+            device_id=(lax.div(to, NGY), lax.rem(to, NGY)), device_id_type=MESH,
         )
 
-    def send_rec(to, carry):
-        @pl.when(to != me)
-        def _():
-            to_device(rec.at[to], recv.at[me], rec_send_sem, rec_recv_sem, to).start()
-
-        return carry
-
-    def send_ret(to, carry):
-        @pl.when(to != me)
-        def _():
-            to_device(ret_send.at[to], ret.at[me], ret_send_sem, ret_recv_sem, to).start()
-
-        return carry
+    mine = lax.div(me, 2)
+    partner = 2 * mine + 1 - lax.rem(me, 2)
+
+    def send_rec(to):
+        to_device(rec.at[to], recv.at[me], rec_send_sem, rec_recv_sem, to).start()
+
+    def send_ret(to):
+        to_device(ret_send.at[to], ret.at[me], ret_send_sem, ret_recv_sem, to).start()
 
     def wait_all(src, dst, send_sem, recv_sem):
         most = pl.ds(0, NDEV - 1)
@@ -496,8 +554,13 @@
         whole.wait_recv()
         whole.wait_send()
 
+    for copy in loads[:5]:
+        copy.wait()
     for half in range(2):
         coef[half, STEPS * 8 : (STEPS + CX) * 8, :] = jnp.zeros((CX * 8, 128), F32)
+        coef[half, ROWS * 8 :, :] = jnp.zeros(((ALL_ROWS - ROWS) * 8, 128), F32)
+        for main in (main_a, main_c):
+            main[half, ROWS * LEV :, :] = jnp.zeros(((ALL_ROWS - ROWS) * LEV, 128), F32)
     for x in range(0, CX, SOLVE_ROWS):
         rows = slice(x, x + SOLVE_ROWS)
         store_level(coef, 0, x, 8, SOLVE_ROWS, zonal[rows, :])
@@ -517,16 +580,19 @@
     for copy in coef_copies + field_copies:
         copy.start()
 
+    for copy in loads[5:10]:
+        copy.wait()
     slot_table(owner, cell, weights, rank, tab, lanes, tiles, cst)
 
     def pack_some(n, carry):
-        j0 = (me // 2 + n * PACK_PAIRS) % (NDEV // 2)
+        j0 = lax.rem(mine + n * (PACK_PAIRS * PAIR_STRIDE), NDEV // 2)
         pack_records(j0, innov, obsw, lanes, tiles, cst, found_ref, rec)
-
-        def send_one(q, carry):
-            return send_rec((2 * j0 + q) % NDEV, carry)
-
-        return lax.fori_loop(0, 2 * PACK_PAIRS, send_one, carry)
+        for q in range(1, PACK_PAIRS):
+            j = lax.rem(j0 + q * PAIR_STRIDE, NDEV // 2)
+            send_rec(2 * j)
+            send_rec(2 * j + 1)
+        send_first(n, j0, partner, send_rec)
+        return carry
 
     lax.fori_loop(0, NDEV // 2 // PACK_PAIRS, pack_some, 0)
     own = pltpu.make_async_copy(rec.at[me], recv.at[me], self_sem)
@@ -536,10 +602,13 @@
         copy.wait()
     unpack_sides(coef_from_high, coef_from_low, coef_side, 8)
     build_faces(coef, coef_side, gy)
+    expand_faces(coef, coef_side, face_x, face_y)
     for copy in field_copies:
         copy.wait()
     unpack_sides(from_high_a, from_low_a, side_a, LEV)
-    diffuse(main_a, side_a, main_b, side_b, coef, coef_side)
+    diffuse(main_a, side_a, field_a, field_b, face_x, face_y)
+
+    loads[10].wait()
 
     def scale(k, carry):
         for x in range(0, CX, 16):
@@ -554,11 +623,12 @@
         return carry
 
     lax.fori_loop(0, LEV, scale, 0)
+    stores[0].start()
     adj[...] = jnp.zeros_like(adj)
 
     own.wait()
     wait_all(rec, recv, rec_send_sem, rec_recv_sem)
-    observe_all(me, recv, field3, adj, ret_send, send_ret)
+    observe_all(mine, partner, recv, field3, adj, ret_send, send_ret)
     own = pltpu.make_async_copy(ret_send.at[me], ret.at[me], self_sem)
     own.start()
 
@@ -579,16 +649,20 @@
     own.wait()
     wait_all(ret_send, ret, ret_send_sem, ret_recv_sem)
     unpack(ret, owner, rank, innov, dep, ret_low, ret_high)
+    stores[1].start()
 
     for copy in adj_copies:
         copy.wait()
     unpack_sides(from_high_c, from_low_c, side_c, LEV)
-    diffuse(main_c, side_c, main_b, side_b, coef, coef_side)
+    diffuse(main_c, side_c, field_a, field_b, face_x, face_y)
     solve_last(main_c, control, vert, mask, upper, inverse, reduced, grad)
+    stores[2].start()
+    for copy in stores:
+        copy.wait()
 
 
 def gradient_call(*args):
-    vmem = pl.BlockSpec(memory_space=pltpu.VMEM)
+    anywhere = pl.BlockSpec(memory_space=pl.ANY)
 
     def field(rows, lanes, lev=LEV):
         shape = (rows * lev, 128)
@@ -597,16 +671,19 @@
     def sides(lev):
         return [field(8, 128, lev), field(8, 128, lev), field(GROUPS, 128, lev), field(GROUPS, 128, lev)]
 
+    outs = (
+        jax.ShapeDtypeStruct((LEV, CX, CY), F32),
+        jax.ShapeDtypeStruct((LEV, PROF), F32),
+        jax.ShapeDtypeStruct((LEV, CX, CY), F32),
+    )
     return pl.pallas_call(
         main_kernel,
-        out_shape=(
-            jax.ShapeDtypeStruct((LEV, CX, CY), F32),
-            jax.ShapeDtypeStruct((LEV, PROF), F32),
-            jax.ShapeDtypeStruct((LEV, CX, CY), F32),
-        ),
-        in_specs=[vmem] * 11,
-        out_specs=(vmem,) * 3,
+        out_shape=outs,
+        in_specs=[anywhere] * len(args),
+        out_specs=(anywhere,) * len(outs),
         scratch_shapes=[
+            *[pltpu.VMEM(a.shape, a.dtype) for a in args + outs],
+            pltpu.SemaphoreType.DMA((len(args) + len(outs),)),
             pltpu.VMEM((NDEV, REC, 128), F32),
             pltpu.VMEM((NDEV, REC, 128), F32),
             pltpu.VMEM((NDEV, 8, 128), F32),
@@ -619,10 +696,11 @@
             pltpu.VMEM((PACK_PAIRS, 40, 128), F32),
             pltpu.VMEM((NDEV // 2, 8, 128), F32),
             pltpu.VMEM((NDEV // 2, 8, 128), F32),
-            field(ROWS, 256, 8), field(SROWS, 128, 8), *sides(8),
-            field(ROWS, 256), field(SROWS, 128),
-            field(ROWS, 256), field(SROWS, 128),
-            field(ROWS, 256), field(SROWS, 128),
+            field(ALL_ROWS, 256, 8), field(SROWS, 128, 8), *sides(8),
+            field(ALL_ROWS, 256), field(SROWS, 128),
+            field(ALL_ROWS, 256), field(SROWS, 128),
+            pltpu.VMEM((SEG + 2, COLS, 128), F32), pltpu.VMEM((SEG + 2, COLS, 128), F32),
+            pltpu.VMEM((SEG + 1, COLS, 128), F32), pltpu.VMEM((SEG, COLS, 128), F32),
             *sides(LEV), *sides(LEV),
             pltpu.VMEM((LEV, CX, CY), F32),
             pltpu.VMEM((LEV, CX, CY), F32),

time: 111 us -> 97.3 us (0.88)
  Pallas kernels: 105 us -> 92.5 us
    pallas_call x1, Pallas kernels: 105 us -> 92.5 us  [gradient_call(): pl.pallas_call(main_kernel, out_shape=outs, in_specs=[anywhere] * len(arg...]
where the time goes in v4:
time: 97.3 us; the launch traced here: 97.1 us
  Pallas kernels  92.5 us (95%)
  local copies, waits for them, and re-layouts  4.02 us (4%)
    pallas_call x1, Pallas kernels, gradient_call(): pl.pallas_call(main_kernel, out_shape=outs, in_specs=[anywhere] * len(arg...  92.5 us
    unnamed x7, local copies, waits for them, and re-layouts  4.02 us

profile of v4, /device:TPU:1, one launch (start us, length us, event | category | flops | bytes accessed | tf_op | source)
XLA Modules:
  0.0 97.1 jit_solution(8391697861314706015)
XLA Ops:
  0.6 92.5 %gradient.1 = (f32[16,64,256]{2,1,0:T(8,128)}, f32[16,2048]{1,0:T(8,128)}, f32[16,64,256]{2,1,0:T(8,128)}) custom-call(f32[16,64,256]{2,1,0:T(8,128)} %control_in.1, f32[16,64,256]{2,1,0:T(8,128)} %sigma_in.1, f32[15,64,256]{2,1,0:T(8,128)} %vert_in.1, f32[64,256]{1,0:T(8,128)} %zonal_in.1, f32[64,256]{1,0:T(8,128)} %merid_in.1, s32[64,256]{1,0:T(8,128)} %mask_in.1, ...), custom_call_target="tpu_custom_call" | custom-call | tf_op jit(solution)/shard_map/gradient/pallas_call | solution.py:679
  93.1 0.0 copy-start.1
  93.1 0.0 copy-start
  93.1 2.4 %copy.17 = f32[16,64,256]{2,1,0:T(8,128)} copy(f32[16,64,256]{2,1,0:T(8,128)} %get-tuple-element.6) | data formatting | bytes 2097152
  95.5 0.0 copy-done.1
  95.5 0.7 copy.18
  96.2 0.0 copy-done
  96.2 1.0 copy.19
Async XLA Ops:
  93.1 2.4 %copy-start.1 = (f32[16,2048]{1,0:T(8,128)S(1)}, f32[16,2048]{1,0:T(8,128)}, u32[]{:S(2)}) copy-start(f32[16,2048]{1,0:T(8,128)} %get-tuple-element.7) | copy-start | bytes 393220
  93.1 3.1 %copy-start = (f32[16,64,256]{2,1,0:T(8,128)S(1)}, f32[16,64,256]{2,1,0:T(8,128)}, u32[]{:S(2)}) copy-start(f32[16,64,256]{2,1,0:T(8,128)} %get-tuple-element.8) | copy-start | bytes 3145732

commit v5 on v4

--- a/solution.py
+++ b/solution.py
@@ -32,8 +32,8 @@
 ALL_ROWS = 8 * SEG
 EDGE = 24
 COLS = CY + 2 * EDGE
-PAIR_STRIDE = 21
 PACK_PAIRS = 8
+WAVES = NDEV // 2 // PACK_PAIRS
 OBSERVE_TILES = 8
 UNPACK_TILES = 2
 
@@ -111,7 +111,7 @@
     below = lax.broadcasted_iota(jnp.int32, (8, 128), 0) // 4
 
     for q in range(PACK_PAIRS):
-        j = lax.rem(j0 + q * PAIR_STRIDE, NDEV // 2)
+        j = lax.rem(j0 + q * WAVES, NDEV // 2)
         lane = jnp.broadcast_to(lanes[pl.ds(j, 1), :], (8, 128))
         tile_of = jnp.broadcast_to(tiles[pl.ds(j, 1), :], (8, 128))
         tile_up = tile_of - below
@@ -130,7 +130,7 @@
         found_ref[q] = jnp.concatenate(found + [place], axis=0)
 
     for q in range(PACK_PAIRS):
-        j = lax.rem(j0 + q * PAIR_STRIDE, NDEV // 2)
+        j = lax.rem(j0 + q * WAVES, NDEV // 2)
         both = found_ref[q]
         place = both[32:36] + both[36:40]
         turned = pltpu.roll(place, 64, axis=1)
@@ -432,7 +432,7 @@
         send(partner)
 
 
-def observe_all(mine, partner, recv, field3, adj, ret_send, send):
+def observe_all(mine, partner, arrived, recv, field3, adj, ret_send, send):
     left = lane_iota(8) < 64
     left_row = lane_iota(1) < 64
     width = OBSERVE_TILES * 128
@@ -440,9 +440,11 @@
     rows_a = lax.broadcasted_iota(jnp.int32, (CX, width), 0).astype(F32)
 
     groups = NDEV // 2 // OBSERVE_TILES
+    assert groups == WAVES
 
     def observe(n, carry):
         pairs = [lax.rem(mine + n + groups * h, NDEV // 2) for h in range(OBSERVE_TILES)]
+        arrived(n)
         parts = []
         for h in range(OBSERVE_TILES):
             one, two = recv[2 * pairs[h]], recv[2 * pairs[h] + 1]
@@ -542,8 +544,8 @@
     mine = lax.div(me, 2)
     partner = 2 * mine + 1 - lax.rem(me, 2)
 
-    def send_rec(to):
-        to_device(rec.at[to], recv.at[me], rec_send_sem, rec_recv_sem, to).start()
+    def rec_copy(to, wave):
+        return to_device(rec.at[to], recv.at[me], rec_send_sem, rec_recv_sem.at[wave], to)
 
     def send_ret(to):
         to_device(ret_send.at[to], ret.at[me], ret_send_sem, ret_recv_sem, to).start()
@@ -585,16 +587,24 @@
     slot_table(owner, cell, weights, rank, tab, lanes, tiles, cst)
 
     def pack_some(n, carry):
-        j0 = lax.rem(mine + n * (PACK_PAIRS * PAIR_STRIDE), NDEV // 2)
+        j0 = lax.rem(mine + NDEV // 2 - n, NDEV // 2)
         pack_records(j0, innov, obsw, lanes, tiles, cst, found_ref, rec)
+        return carry
+
+    def send_some(n, carry):
+        j0 = lax.rem(mine + NDEV // 2 - n, NDEV // 2)
+
+        def send(to):
+            rec_copy(to, n).start()
+
         for q in range(1, PACK_PAIRS):
-            j = lax.rem(j0 + q * PAIR_STRIDE, NDEV // 2)
-            send_rec(2 * j)
-            send_rec(2 * j + 1)
-        send_first(n, j0, partner, send_rec)
-        return carry
-
-    lax.fori_loop(0, NDEV // 2 // PACK_PAIRS, pack_some, 0)
+            j = lax.rem(j0 + q * WAVES, NDEV // 2)
+            send(2 * j)
+            send(2 * j + 1)
+        send_first(n, j0, partner, send)
+        return carry
+
+    lax.fori_loop(0, WAVES, pack_some, 0)
     own = pltpu.make_async_copy(rec.at[me], recv.at[me], self_sem)
     own.start()
 
@@ -605,6 +615,7 @@
     expand_faces(coef, coef_side, face_x, face_y)
     for copy in field_copies:
         copy.wait()
+    lax.fori_loop(0, WAVES, send_some, 0)
     unpack_sides(from_high_a, from_low_a, side_a, LEV)
     diffuse(main_a, side_a, field_a, field_b, face_x, face_y)
 
@@ -627,8 +638,23 @@
     adj[...] = jnp.zeros_like(adj)
 
     own.wait()
-    wait_all(rec, recv, rec_send_sem, rec_recv_sem)
-    observe_all(mine, partner, recv, field3, adj, ret_send, send_ret)
+
+    def arrived(n):
+        def some(count):
+            at = pl.ds(0, count)
+            to_device(rec.at[at], recv.at[at], rec_send_sem, rec_recv_sem.at[n], me).wait_recv()
+
+        @pl.when(n == 0)
+        def _():
+            some(2 * PACK_PAIRS - 1)
+
+        @pl.when(n > 0)
+        def _():
+            some(2 * PACK_PAIRS)
+
+    observe_all(mine, partner, arrived, recv, field3, adj, ret_send, send_ret)
+    most = pl.ds(0, NDEV - 1)
+    to_device(rec.at[most], recv.at[most], rec_send_sem, rec_recv_sem.at[0], me).wait_send()
     own = pltpu.make_async_copy(ret_send.at[me], ret.at[me], self_sem)
     own.start()
 
@@ -707,7 +733,7 @@
             pltpu.VMEM((LEV, CX, CY), F32),
             pltpu.VMEM((LEV * CX, 3 * CY), BF16),
             pltpu.VMEM((LEV * CX, CY), F32),
-            pltpu.SemaphoreType.DMA, pltpu.SemaphoreType.DMA, pltpu.SemaphoreType.DMA, pltpu.SemaphoreType.DMA,
+            pltpu.SemaphoreType.DMA, pltpu.SemaphoreType.DMA((WAVES,)), pltpu.SemaphoreType.DMA, pltpu.SemaphoreType.DMA,
             pltpu.SemaphoreType.DMA,
             pltpu.SemaphoreType.DMA((3, 8)), pltpu.SemaphoreType.DMA((3, 8)),
         ],

time: 97.3 us -> 89.3 us (0.918)
  Pallas kernels: 92.5 us -> 84.5 us
    pallas_call x1, Pallas kernels: 92.5 us -> 84.5 us  [gradient_call(): pl.pallas_call(main_kernel, out_shape=outs, in_specs=[anywhere] * len(arg...]
where the time goes in v5:
time: 89.3 us; the launch traced here: 89.2 us
  Pallas kernels  84.5 us (95%)
  local copies, waits for them, and re-layouts  4.02 us (5%)
    pallas_call x1, Pallas kernels, gradient_call(): pl.pallas_call(main_kernel, out_shape=outs, in_specs=[anywhere] * len(arg...  84.5 us
    unnamed x7, local copies, waits for them, and re-layouts  4.02 us

profile of v5, /device:TPU:1, one launch (start us, length us, event | category | flops | bytes accessed | tf_op | source)
XLA Modules:
  0.0 89.2 jit_solution(2294570993665466123)
XLA Ops:
  0.6 84.5 %gradient.1 = (f32[16,64,256]{2,1,0:T(8,128)}, f32[16,2048]{1,0:T(8,128)}, f32[16,64,256]{2,1,0:T(8,128)}) custom-call(f32[16,64,256]{2,1,0:T(8,128)} %control_in.1, f32[16,64,256]{2,1,0:T(8,128)} %sigma_in.1, f32[15,64,256]{2,1,0:T(8,128)} %vert_in.1, f32[64,256]{1,0:T(8,128)} %zonal_in.1, f32[64,256]{1,0:T(8,128)} %merid_in.1, s32[64,256]{1,0:T(8,128)} %mask_in.1, ...), custom_call_target="tpu_custom_call" | custom-call | tf_op jit(solution)/shard_map/gradient/pallas_call | solution.py:705
  85.1 0.0 copy-start.1
  85.1 0.0 copy-start
  85.1 2.4 %copy.17 = f32[16,64,256]{2,1,0:T(8,128)} copy(f32[16,64,256]{2,1,0:T(8,128)} %get-tuple-element.6) | data formatting | bytes 2097152
  87.5 0.0 copy-done.1
  87.5 0.7 copy.18
  88.2 0.0 copy-done
  88.2 1.0 %copy.19 = f32[16,64,256]{2,1,0:T(8,128)} copy(f32[16,64,256]{2,1,0:T(8,128)S(1)} %copy-done) | data formatting | bytes 2097152
Async XLA Ops:
  85.1 2.4 %copy-start.1 = (f32[16,2048]{1,0:T(8,128)S(1)}, f32[16,2048]{1,0:T(8,128)}, u32[]{:S(2)}) copy-start(f32[16,2048]{1,0:T(8,128)} %get-tuple-element.7) | copy-start | bytes 393220
  85.1 3.1 %copy-start = (f32[16,64,256]{2,1,0:T(8,128)S(1)}, f32[16,64,256]{2,1,0:T(8,128)}, u32[]{:S(2)}) copy-start(f32[16,64,256]{2,1,0:T(8,128)} %get-tuple-element.8) | copy-start | bytes 3145732

commit v6 on v5

--- a/solution.py
+++ b/solution.py
@@ -27,7 +27,7 @@
 SROWS = 96
 GROUPS = 12
 REC = 18
-DIFFUSE_TILES = 4
+DIFFUSE_TILES = 8
 SEG = 11
 ALL_ROWS = 8 * SEG
 EDGE = 24
@@ -744,11 +744,50 @@
     )(*args)
 
 
+def settle_kernel(*refs):
+    count = (len(refs) - 2) // 3
+    sources, targets, held = refs[:count], refs[count : 2 * count], refs[2 * count : 3 * count]
+    moves = []
+    for n in range(count):
+        half = LEV // 2
+        for part in range(2):
+            at = pl.ds(part * half, half)
+            sem = 2 * n + part
+            moves.append((
+                pltpu.make_async_copy(sources[n].at[at], held[n].at[at], refs[-2].at[sem]),
+                pltpu.make_async_copy(held[n].at[at], targets[n].at[at], refs[-1].at[sem]),
+            ))
+    for load, _ in moves:
+        load.start()
+    for load, store in moves:
+        load.wait()
+        store.start()
+    for _, store in moves:
+        store.wait()
+
+
+def settle(*arrays):
+    anywhere = pl.BlockSpec(memory_space=pl.ANY)
+    return pl.pallas_call(
+        settle_kernel,
+        out_shape=tuple(jax.ShapeDtypeStruct(a.shape, a.dtype) for a in arrays),
+        in_specs=[anywhere] * len(arrays),
+        out_specs=(anywhere,) * len(arrays),
+        scratch_shapes=[
+            *[pltpu.VMEM(a.shape, a.dtype) for a in arrays],
+            pltpu.SemaphoreType.DMA((2 * len(arrays),)),
+            pltpu.SemaphoreType.DMA((2 * len(arrays),)),
+        ],
+        compiler_params=pltpu.CompilerParams(vmem_limit_bytes=VMEM_LIMIT),
+        name="settle",
+    )(*arrays)
+
+
 def shards(control, sigma, vert_diff, zonal_diff, merid_diff, ocean_mask, owner, cell, interp_weights, innovation, obs_weight):
-    return gradient_call(
+    return settle(*gradient_call(
         control, sigma, vert_diff, zonal_diff, merid_diff, ocean_mask,
         owner.reshape(TILES, 128), cell.reshape(TILES, 128), interp_weights, innovation, obs_weight,
-    )
+    ))
 
 
 def solution(mesh):

time: 89.3 us -> 87.1 us (0.975)
  local copies, waits for them, and re-layouts: 4.02 us -> 0 us
  Pallas kernels: 84.5 us -> 86.3 us
    unnamed x7 -> x0, local copies, waits for them, and re-layouts: 4.02 us -> none
    pallas_call x0 -> x1, Pallas kernels: none -> 2.5 us  [settle(): pl.pallas_call(settle_kernel, out_shape=tuple((jax.ShapeDtypeStruct(a.sha...]
where the time goes in v6:
time: 87.1 us; the launch traced here: 86.9 us
  Pallas kernels  86.3 us (99%)
    pallas_call x1, Pallas kernels, gradient_call(): pl.pallas_call(main_kernel, out_shape=outs, in_specs=[anywhere] * len(arg...  83.8 us
    pallas_call x1, Pallas kernels, settle(): pl.pallas_call(settle_kernel, out_shape=tuple((jax.ShapeDtypeStruct(a.sha...  2.5 us

profile of v6, /device:TPU:1, one launch (start us, length us, event | category | flops | bytes accessed | tf_op | source)
XLA Modules:
  0.0 86.9 jit_solution(3409241662076242023)
XLA Ops:
  0.6 83.8 %gradient.1 = (f32[16,64,256]{2,1,0:T(8,128)}, f32[16,2048]{1,0:T(8,128)}, f32[16,64,256]{2,1,0:T(8,128)}) custom-call(f32[16,64,256]{2,1,0:T(8,128)} %control_in.1, f32[16,64,256]{2,1,0:T(8,128)} %sigma_in.1, f32[15,64,256]{2,1,0:T(8,128)} %vert_in.1, f32[64,256]{1,0:T(8,128)} %zonal_in.1, f32[64,256]{1,0:T(8,128)} %merid_in.1, s32[64,256]{1,0:T(8,128)} %mask_in.1, ...), custom_call_target="tpu_custom_call" | custom-call | tf_op jit(solution)/shard_map/gradient/pallas_call | solution.py:705
  84.4 2.5 %settle.1 = (f32[16,64,256]{2,1,0:T(8,128)}, f32[16,2048]{1,0:T(8,128)}, f32[16,64,256]{2,1,0:T(8,128)}) custom-call(f32[16,64,256]{2,1,0:T(8,128)} %get-tuple-element.6.refs_0_, f32[16,2048]{1,0:T(8,128)} %get-tuple-element.7.refs_1_, f32[16,64,256]{2,1,0:T(8,128)} %get-tuple-element.8.refs_2_), custom_call_target="tpu_custom_call" | custom-call | tf_op jit(solution)/shard_map/settle/pallas_call | solution.py:771
